TPU v7x, 256 devices: a whole 4x4x8 slice. The times are simulated.
256 devices in a mesh: virt: 64 (over z, y, core), rep: 4 (over x).
Axes of the slice: x: 4, y: 4, z: 8, core: 2. Of those that a mesh axis runs over, the one named last changes fastest.
Arguments:
- t2_packed: float32 [256, 921600], P(None, ('virt', 'rep')), may hold values from -6 to 6
- w_packed: float32 [921600, 512], P(('virt', 'rep')), may hold values from -0.015625 to 0.015625
- pair_list: int32 [2, 921600], P(None, ('virt', 'rep')), may hold values from 0 to 959, as said below
- block_starts: int32 [8], replicated, may hold values from 0 to 921599, as said below
- singles: float32 [120, 960], replicated, may hold values from -3 to 3
- row_pairs: int32 [8, 256, 2], replicated, may hold values from 0 to 119, as said below
- col_pairs: int32 [8, 512, 2], P(None, 'rep'), may hold values from 0 to 959, as said below
- t2_slab: float32 [8, 256, 512], P(None, 'virt', 'rep'), may hold values from -6 to 6
- w_hole: float32 [8, 256, 256], P(None, 'virt'), may hold values from -0.375 to 0.375
- driver: float32 [8, 256, 512], P(None, 'virt', 'rep'), may hold values from -6 to 6
- occ_energy: float32 [120], replicated, may hold values from -2 to -0.5
- vir_energy: float32 [960], replicated, may hold values from 0.2 to 3
Outputs:
- t2_new: float32 [8, 256, 512], P(None, 'virt', 'rep')
Inputs may be any that keep to these rules, and one draw needn't show every extreme that they name: Column p of pair_list holds the two virtual orbitals of packed pair p; every ordered pair of virtual orbitals occurs once, grouped into irrep blocks that begin at block_starts. block_starts[0] is 0 and the starts rise; every block holds at least 28800 pairs. `row_pairs`: the irreps of the two occupied orbitals of a slot of group h multiply to h. `col_pairs`: the irreps of the two virtual orbitals of a slab pair of group h multiply to h.
All inputs are finite; a program needn't handle non-finite values.
Results may differ from a plain program's by a relative error of at most 0.0003.
Values sent between devices are 32-bit elements; how exact they have to be, the bound alone decides.
A program may use at most 128 MiB of HBM per device.

v0:
```python
import jax
import jax.numpy as jnp
from jax import lax
from jax.sharding import PartitionSpec as P


def block_of(positions, block_starts):
    return jnp.sum((positions[:, None] >= block_starts[None, 1:]).astype(jnp.int32), axis=1)


def pair_terms(singles, row_pairs, group, orbit_c, orbit_d):
    left_rows = jnp.take(singles, row_pairs[group, :, 0], axis=0)
    right_rows = jnp.take(singles, row_pairs[group, :, 1], axis=0)
    return jnp.take(left_rows, orbit_c, axis=1) * jnp.take(right_rows, orbit_d, axis=1)


def ladder_pieces(t2_piece, w_piece, pair_piece, positions, block_starts, singles, row_pairs):
    blocks = block_of(positions, block_starts)
    first_block = blocks[0]
    final_block = blocks[blocks.shape[0] - 1]

    def single_block(unused):
        terms = pair_terms(singles, row_pairs, first_block, pair_piece[0], pair_piece[1])
        whole_part = jnp.dot(
            t2_piece + terms,
            w_piece,
            precision=lax.Precision.HIGHEST,
            preferred_element_type=jnp.float32,
        )
        return (whole_part, jnp.zeros_like(whole_part))

    def split_blocks(unused):
        in_first = (blocks == first_block)[None, :]
        first_terms = pair_terms(singles, row_pairs, first_block, pair_piece[0], pair_piece[1])
        final_terms = pair_terms(singles, row_pairs, final_block, pair_piece[0], pair_piece[1])
        dressed = t2_piece + jnp.where(in_first, first_terms, final_terms)
        empty_like = jnp.zeros_like(dressed)
        first_part = jnp.dot(
            jnp.where(in_first, dressed, empty_like),
            w_piece,
            precision=lax.Precision.HIGHEST,
            preferred_element_type=jnp.float32,
        )
        second_part = jnp.dot(
            jnp.where(in_first, empty_like, dressed),
            w_piece,
            precision=lax.Precision.HIGHEST,
            preferred_element_type=jnp.float32,
        )
        return (first_part, second_part)

    first_part, second_part = lax.cond(first_block == final_block, single_block, split_blocks, 0)
    return (first_block, final_block, first_part, second_part)


def slab_dressing(t2_slab, singles, rows, cols):
    left_rows = jnp.take(singles, rows[:, :, 0], axis=0)
    right_rows = jnp.take(singles, rows[:, :, 1], axis=0)
    target = (rows.shape[0], rows.shape[1], cols.shape[1])
    index_a = jnp.broadcast_to(cols[:, None, :, 0], target)
    index_b = jnp.broadcast_to(cols[:, None, :, 1], target)
    return t2_slab + jnp.take_along_axis(left_rows, index_a, axis=2) * jnp.take_along_axis(
        right_rows, index_b, axis=2
    )


def denominators(rows, cols, occ_energy, vir_energy):
    virtual_sum = vir_energy[cols[:, None, :, 0]] + vir_energy[cols[:, None, :, 1]]
    return virtual_sum - occ_energy[rows[:, :, None, 0]] - occ_energy[rows[:, :, None, 1]]


def body(
    t2_packed,
    w_packed,
    pair_list,
    block_starts,
    singles,
    row_pairs,
    col_pairs,
    t2_slab,
    w_hole,
    driver,
    occ_energy,
    vir_energy,
):
    columns = t2_packed.shape[1]
    rep_count = lax.axis_size("rep")
    segment = lax.axis_index("virt") * rep_count + lax.axis_index("rep")
    positions = segment * columns + jnp.arange(columns, dtype=jnp.int32)
    first_block, final_block, first_part, second_part = ladder_pieces(
        t2_packed, w_packed, pair_list, positions, block_starts, singles, row_pairs
    )
    groups = jnp.arange(row_pairs.shape[0], dtype=jnp.int32)
    first_weight = (groups == first_block).astype(jnp.float32)[:, None, None]
    final_weight = (groups == final_block).astype(jnp.float32)[:, None, None]
    spread = first_weight * first_part[None] + final_weight * second_part[None]
    partly = lax.psum_scatter(spread, "rep", scatter_dimension=2, tiled=True)
    ladder = lax.psum_scatter(partly, "virt", scatter_dimension=1, tiled=True)
    local_count = driver.shape[1]
    local_rows = lax.dynamic_slice_in_dim(
        row_pairs, lax.axis_index("virt") * local_count, local_count, 1
    )
    slab_dressed = slab_dressing(t2_slab, singles, local_rows, col_pairs)
    hole_term = jnp.einsum(
        "hrk,hkq->hrq",
        w_hole,
        lax.all_gather(slab_dressed, "virt", axis=1, tiled=True),
        precision=lax.Precision.HIGHEST,
    )
    denominator = denominators(local_rows, col_pairs, occ_energy, vir_energy)
    return (driver + ladder + hole_term) / denominator


def solution(mesh):
    in_specs = (
        P(None, ("virt", "rep")),
        P(("virt", "rep"), None),
        P(None, ("virt", "rep")),
        P(),
        P(),
        P(),
        P(None, "rep", None),
        P(None, "virt", "rep"),
        P(None, "virt", None),
        P(None, "virt", "rep"),
        P(),
        P(),
    )
    out_specs = P(None, "virt", "rep")
    return jax.shard_map(body, mesh=mesh, in_specs=in_specs, out_specs=out_specs, check_vma=False)
```

profile of v0, /device:TPU:2, one launch (start us, length us, event | category | flops | bytes accessed | tf_op | source)
XLA Modules:
  0.0 413.1 jit_solution(10220776208602688177)
XLA Ops:
  7.4 0.7 slice.39
  8.1 0.1 convert_reduce_fusion
  8.2 0.6 fusion.40
  10.1 1.3 compare_convert_fusion
  11.4 53.5 %conditional.1 = (f32[256,512]{1,0:T(8,128)}, f32[256,512]{1,0:T(8,128)S(1)}) conditional(s32[]{:T(128)} %convert_element_type.22, (s32[]{:T(128)}, s32[3600]{0:T(1024)S(1)}, s32[8,256,2]{1,2,0:T(2,128)}, f32[120,960]{1,0:T(8,128)}, s32[2,3600]{1,0:T(2,128)}, /*index=5*/s32[]{:T(128)}, f32[256,3600]{0,1:T(8,128)}, f32[3600,512]{1,0:T(8,128)}) %tuple.17, ...), branch_computations={%region_1.4_spmd, %region_2.5_spmd} | conditional | flops 11334909952 | bytes 100681560 | solution.py:52
  21.5 0.8 constant_dynamic-slice_fusion.5
  22.3 2.6 gather_fusion.8
  24.9 0.1 broadcast_select_fusion.5
  25.1 0.3 copy.75
  25.4 0.3 copy-done.7
  25.7 0.1 slice_reduce_fusion.3
  25.8 10.0 %gather_fusion.9 = f32[3600,256]{1,0:T(8,128)} fusion(f32[256,960]{0,1:T(8,128)S(1)} %copy.75, s32[4096]{0:T(1024)S(1)} %pad_clamp_fusion.7), kind=kCustom, calls=%fused_computation.12.clone | custom fusion | bytes 7387200 | tf_op jit(solution)/shard_map/cond/branch_1_fun/jit(_take)/gather | solution.py:14
  35.8 1.1 gather_fusion.10
  36.9 1.1 broadcast_select_fusion.4
  38.0 1.5 copy.76
  39.6 10.0 %gather_fusion.11 = f32[3600,256]{1,0:T(8,128)} fusion(f32[256,960]{0,1:T(8,128)S(1)} %copy.76, s32[4096]{0:T(1024)S(1)} %pad_clamp_fusion.6), kind=kCustom, calls=%fused_computation.13.clone | custom fusion | bytes 7387200 | tf_op jit(solution)/shard_map/cond/branch_1_fun/jit(_take)/gather | solution.py:14
  49.6 14.9 %fusion.13 = f32[256,512]{1,0:T(8,128)} fusion(f32[3600,512]{1,0:T(8,128)} %get-tuple-element.50, f32[256,3600]{0,1:T(8,128)} %get-tuple-element.45, f32[3600,256]{1,0:T(8,128)} %gather_fusion.11, f32[3600,256]{1,0:T(8,128)} %gather_fusion.9, pred[3600]{0:T(1024)(128)(4,1)S(1)} %get-tuple-element.83, pred[3600]{0:T(1024)(128)(4,1)S(1)} %get-tuple-element.84), kind=kOutput, calls=%fused_computation.65 | convolution fusion | flops 5665996800 | bytes 18963488 | tf_op jit(solution)/shard_map/cond/branch_1_fun/dot_general | solution.py:24
  64.9 3.7 multiply_add_fusion
  68.6 0.0 all-gather.2.cloned.1.call-start
  68.7 0.1 fusion.38
  68.8 0.1 copy.79
  68.9 0.1 copy.81
  68.9 0.1 reshape.350
  69.0 0.6 gather_fusion.16
  69.7 0.1 copy.80
  69.8 0.1 copy.82
  69.9 0.1 copy.84
  70.0 0.1 reshape.359
  70.1 0.6 gather_fusion.18
  70.8 0.1 copy.83
  70.9 0.1 broadcast_select_fusion.7
  71.0 40.3 %gather_fusion.17 = f32[4096]{0:T(1024)S(1)} fusion(f32[8,4,960]{2,1,0:T(4,128)S(1)} %broadcast_select_fusion.7, s32[4096]{0:T(1024)S(1)} %bitcast.79), kind=kCustom, calls=%fused_computation.3.clone | custom fusion | bytes 81920 | tf_op jit(solution)/shard_map/jit(take_along_axis)/gather | solution.py:62
  111.4 0.1 broadcast_select_fusion.6
  111.5 40.3 %gather_fusion.19 = f32[4096]{0:T(1024)S(1)} fusion(f32[8,4,960]{2,1,0:T(4,128)S(1)} %broadcast_select_fusion.6, s32[4096]{0:T(1024)S(1)} %bitcast.80), kind=kCustom, calls=%fused_computation.15.clone | custom fusion | bytes 81920 | tf_op jit(solution)/shard_map/jit(take_along_axis)/gather | solution.py:62
  151.8 0.6 copy.85
  152.5 0.0 reduce-scatter.5.cloned.1.call-start
  152.6 0.5 reduce-scatter.5.cloned.1.call-update
  153.1 0.1 reshape.273
  153.2 0.7 gather_fusion.14
  153.9 0.1 sub.26
  153.9 0.1 reshape.281
  154.0 0.7 gather_fusion.15
  154.7 0.1 sub.29
  154.9 4.5 %gather_fusion.12 = f32[1024]{0:T(1024)S(1)} fusion(f32[960]{0:T(1024)S(1)} %copy-done.2, s32[1024]{0:T(1024)S(1)} %fusion.35), kind=kCustom, calls=%fused_computation.16 | custom fusion | bytes 12288 | tf_op jit(solution)/shard_map/gather | solution.py:68
  159.4 4.5 %gather_fusion.13 = f32[1024]{0:T(1024)S(1)} fusion(f32[960]{0:T(1024)S(1)} %copy-done.2, s32[1024]{0:T(1024)S(1)} %fusion.37), kind=kCustom, calls=%fused_computation.17 | custom fusion | bytes 12288 | tf_op jit(solution)/shard_map/gather | solution.py:68
  164.0 97.2 %all-gather.2.cloned.1.call-done = f32[8,256,128]{2,0,1:T(8,128)} async-done(((f32[8,4,128]{2,0,1:T(8,128)}), f32[8,256,128]{2,0,1:T(8,128)}) %all-gather.2.cloned.1.call-update) | async-done | bytes 1048592 | tf_op jit(solution)/shard_map/all_gather | solution.py:107
  261.2 141.5 %reduce-scatter.5.cloned.1.call-done = f32[8,4,128]{2,0,1:T(8,128)} async-done(((f32[8,256,128]{2,0,1:T(8,128)}), f32[8,4,128]{2,0,1:T(8,128)}) %reduce-scatter.5.cloned.1.call-update) | async-done | bytes 16400 | tf_op jit(solution)/shard_map/reduce_scatter | solution.py:98
  402.7 2.6 fusion.23
  (54 shorter events, 0.5 us)
Async XLA Ops:
  7.4 395.3 %copy-start = (f32[8,4,256]{2,1,0:T(4,128)S(1)}, f32[8,4,256]{2,1,0:T(4,128)}, u32[]{:S(2)}) copy-start(f32[8,4,256]{2,1,0:T(4,128)} %param.30) | copy-start | bytes 98308
  7.4 145.2 %reduce-scatter.3.cloned.1.call-start = ((), (), s32[]{:S(2)}) async-start(), calls=%async_computation.2 | async-start | bytes 5242880 | tf_op jit(solution)/shard_map/reduce_scatter | solution.py:97
  24.9 0.8 copy-start.7
  25.8 10.0 %copy-start.5 = (f32[120,960]{1,0:T(8,128)S(1)}, f32[120,960]{1,0:T(8,128)}, u32[]{:S(2)}) copy-start(f32[120,960]{1,0:T(8,128)} %get-tuple-element.46) | copy-start | bytes 1382404 | tf_op jit(solution)/shard_map/cond
  64.8 3.8 copy-start.10
  64.8 4.2 %copy-start.3 = (f32[120,960]{1,0:T(8,128)S(1)}, f32[120,960]{1,0:T(8,128)}, u32[]{:S(2)}) copy-start(f32[120,960]{1,0:T(8,128)} %param.26) | copy-start | bytes 1382404
  68.6 2.3 copy-start.11
  68.6 192.6 %all-gather.2.cloned.1.call-start = ((), (), s32[]{:S(2)}) async-start(), calls=%async_computation.4 | async-start | bytes 1064960 | tf_op jit(solution)/shard_map/all_gather | solution.py:107
  111.5 40.3 %copy-start.9 = (f32[8,4,128]{2,1,0:T(4,128)S(1)}, f32[8,4,128]{2,1,0:T(4,128)}, u32[]{:S(2)}) copy-start(f32[8,4,128]{2,1,0:T(4,128)} %param.29) | copy-start | bytes 49156
  151.8 1.4 copy-start.1
  152.5 250.2 %reduce-scatter.5.cloned.1.call-start = ((), (), s32[]{:S(2)}) async-start(), calls=%async_computation.3 | async-start | bytes 1064960 | tf_op jit(solution)/shard_map/reduce_scatter | solution.py:98
  153.2 1.7 copy-start.2
  154.9 247.8 %copy-start.8 = (f32[8,4,128]{2,1,0:T(4,128)S(1)}, f32[8,4,128]{2,1,0:T(4,128)}, u32[]{:S(2)}) copy-start(f32[8,4,128]{2,1,0:T(4,128)} %param.31) | copy-start | bytes 49156
Sparse Core Ops, SparseCore 0:
  68.7 80.1 reduce-scatter.2
Sparse Core Ops, SparseCore 1:
  152.6 108.6 all-gather.1
  265.6 137.1 reduce-scatter.4
where the time goes:
time: 421 us; the launch traced here: 413 us
  waiting for transfers between devices  239 us (57%)
  local copies, waits for them, and re-layouts  122 us (29%)
  matrix products  17.5 us (4%)
  between operations  16.8 us (4%)
  loops' own time  10.5 us (2%)
  other arithmetic  6.88 us (2%)
    reduce_scatter x1, waiting for transfers between devices, body(): ladder = lax.psum_scatter(partly, 'virt', scatter_dimension=1, tiled=True)  142 us
    all_gather x1, waiting for transfers between devices, body(): lax.all_gather(slab_dressed, 'virt', axis=1, tiled=True)  97.2 us
    gather x1, local copies, waits for them, and re-layouts, slab_dressing(): jnp.take_along_axis(left_rows, index_a, axis=2)  40.3 us
    gather x1, local copies, waits for them, and re-layouts, slab_dressing(): jnp.take_along_axis(right_rows, index_b, axis=2)  40.3 us
    dot_general x1, matrix products, single_block(): jnp.dot(t2_piece + terms, w_piece, precision=lax.Precision.HIGHEST, prefe...  14.9 us
    another operation x1, loops' own time, ladder_pieces(): lax.cond(first_block == final_block, single_block, split_blocks, 0)  10.5 us
    gather x1, local copies, waits for them, and re-layouts, pair_terms(): jnp.take(right_rows, orbit_d, axis=1)  9.99 us
    gather x1, local copies, waits for them, and re-layouts, pair_terms(): jnp.take(left_rows, orbit_c, axis=1) * jnp.take(right_rows, orbit_d, axis=1)  9.99 us
  transfers between devices with their start and end apart: 3, of which 2 were waited for; matrix products, arithmetic and copies ran while one was open for 23% of the time, Pallas kernels for 0%

commit v1 on v0

v1 whole, which is shorter than its diff:
```python
import jax
import jax.numpy as jnp
from jax import lax
from jax.experimental import pallas as pl
from jax.experimental.pallas import tpu as pltpu
from jax.sharding import PartitionSpec as P

MESH = pl.DeviceIdType.MESH
F32 = jnp.float32
BF16 = jnp.bfloat16
I32 = jnp.int32

GROUPS = 8
OCC = 120
VIRT = 960
ROWS = 256
COLS = 512
PIECE = 3600
STEP = 720
STEPS = PIECE // STEP
NZ = 8
NY = 4
NX = 4
PLACES = NZ * NY
PLACE = 8 * PIECE
HALF = PLACES // 2


def split(value):
    high = value.astype(BF16)
    return high, (value - high.astype(F32)).astype(BF16)


def block_at(starts, position):
    block = jnp.int32(0)
    for h in range(1, GROUPS):
        block += (position >= starts[h]).astype(I32)
    return block


def over_rows(left, right):
    return lax.dot_general(left, right, (((0,), (0,)), ((), ())), preferred_element_type=F32)


def ladder_kernel(
    starts, singles, pairs, rows, t2_hbm, w_hbm, out_a, out_b, t2, w, pair, padded, table, select, sems
):
    copies = []
    for k in range(STEPS):
        copies.append(
            (
                pltpu.make_async_copy(t2_hbm.at[k], t2.at[k], sems.at[0, k]),
                pltpu.make_async_copy(w_hbm.at[k], w.at[k], sems.at[1, k]),
            )
        )
        for copy in copies[-1]:
            copy.start()
    segment = lax.axis_index("virt") * NX + lax.axis_index("rep")
    place = lax.axis_index("virt") // 2
    block_a = block_at(starts, place * PLACE)
    block_b = block_at(starts, place * PLACE + PLACE - 1)
    count = jnp.clip(starts[block_b] - segment * PIECE, 0, PIECE)
    mixed = jnp.minimum(count // STEP, STEPS - 1)

    padded[...] = jnp.zeros_like(padded)
    padded[0:OCC, 0:VIRT] = singles[...]
    high, low = split(padded[...].T)
    table[:, 0:128] = high
    table[:, 128:256] = low
    for k in range(STEPS):
        part = pairs[:, k * STEP : (k + 1) * STEP]
        pair[k] = jnp.concatenate([part, jnp.zeros((6, STEP), I32)], axis=0).T
    orbit = lax.broadcasted_iota(I32, (128, ROWS), 0)
    for s, block in enumerate((block_a, block_b)):
        for side in range(2):
            hit = (orbit == rows[block, side : side + 1, :]).astype(F32)
            select[s, side] = jnp.concatenate([hit, hit], axis=0).astype(BF16)
    out_a[...] = jnp.zeros_like(out_a)
    out_b[...] = jnp.zeros_like(out_b)

    def gathered(k, side):
        index = pair[k][:, side : side + 1]
        hit = (lax.broadcasted_iota(I32, (STEP, 1024), 1) == index).astype(BF16)
        return jnp.dot(hit, table[...], preferred_element_type=F32).astype(BF16)

    def dressed(k, orbit_c, orbit_d, select_i, select_j):
        left = jnp.dot(orbit_c, select_i, preferred_element_type=F32)
        right = jnp.dot(orbit_d, select_j, preferred_element_type=F32)
        return t2[k] + left * right

    def product(value, k):
        value_high, value_low = split(value)
        w_high, w_low = split(w[k])
        return (
            over_rows(value_high, w_high) + over_rows(value_high, w_low) + over_rows(value_low, w_high)
        )

    def step(k, carry):
        pltpu.make_async_copy(t2_hbm.at[k], t2.at[k], sems.at[0, k]).wait()
        pltpu.make_async_copy(w_hbm.at[k], w.at[k], sems.at[1, k]).wait()
        in_a = k < mixed
        value = dressed(
            k,
            gathered(k, 0),
            gathered(k, 1),
            jnp.where(in_a, select[0, 0], select[1, 0]),
            jnp.where(in_a, select[0, 1], select[1, 1]),
        )
        part = product(value, k)
        out_a[...] += part * jnp.where(k < mixed, 1.0, 0.0)
        out_b[...] += part * jnp.where(k > mixed, 1.0, 0.0)
        return carry

    lax.fori_loop(0, STEPS, step, 0)
    orbit_c = gathered(mixed, 0)
    orbit_d = gathered(mixed, 1)
    mask = lax.broadcasted_iota(I32, (STEP, ROWS), 0) < count - mixed * STEP
    value_a = jnp.where(mask, dressed(mixed, orbit_c, orbit_d, select[0, 0], select[0, 1]), 0.0)
    out_a[...] += product(value_a, mixed)
    value_b = jnp.where(mask, 0.0, dressed(mixed, orbit_c, orbit_d, select[1, 0], select[1, 1]))
    out_b[...] += product(value_b, mixed)


def lookup(columns, index):
    low = index & 127
    tile = index >> 7
    found = jnp.zeros((8, 128), F32)
    for t in range(8):
        piece = jnp.take_along_axis(
            columns[:, 128 * t : 128 * (t + 1)], low, axis=1, mode="promise_in_bounds"
        )
        found = jnp.where(tile == t, piece, found)
    return found


def exchange_kernel(
    starts,
    part_a,
    part_b,
    singles,
    rows,
    cols,
    t2_slab,
    w_hole,
    driver,
    occ,
    vir,
    out,
    mine,
    give,
    got,
    ring1,
    ring2,
    recv,
    slab_send,
    slab_recv,
    slab_all,
    hole_send,
    hole_recv,
    core_sems,
    ring_sems,
    all_sems,
    h1_sems,
    h2_sems,
    h3_sems,
):
    virt = lax.axis_index("virt")
    x = lax.axis_index("rep")
    core = lax.rem(virt, 2)
    place = virt // 2
    y = lax.rem(place, NY)
    z = place // NY
    xp = lax.rem(x + 1, NX)
    xo = lax.rem(x + 2, NX)
    xm = lax.rem(x + 3, NX)

    def device(place_to, core_to):
        return (place_to * 2 + core_to, x)

    barrier = pltpu.get_barrier_semaphore()

    def greet(target):
        pl.semaphore_signal(barrier, inc=1, device_id=target, device_id_type=MESH)

    greet(device(place, 1 - core))
    greet((virt, xp))
    greet((virt, xm))

    def greet_place(d, carry):
        greet(device(lax.rem(place + d, PLACES), core))
        return carry

    lax.fori_loop(1, PLACES, greet_place, 0)
    for d in range(1, NY):
        greet(device(z * NY + lax.rem(y + d, NY), 1 - core))

    upper = lax.broadcasted_iota(I32, (PLACES, 8, 128), 1) < 4
    for q in range(NX):
        a = part_a[:, 128 * q : 128 * (q + 1)].reshape(PLACES, 8, 128)
        b = part_b[:, 128 * q : 128 * (q + 1)].reshape(PLACES, 8, 128)
        tile0 = jnp.where(upper, a, pltpu.roll(b, 4, 1))
        tile1 = jnp.where(upper, pltpu.roll(a, 4, 1), b)
        mine[q] = jnp.where(core == 0, tile0, tile1)
        give[q] = jnp.where(core == 0, tile1, tile0)

    pl.semaphore_wait(barrier, 2 + PLACES - 1 + 1 + NY - 1)

    def core_copy(q):
        return pltpu.make_async_remote_copy(
            src_ref=give.at[q],
            dst_ref=got.at[q],
            send_sem=core_sems.at[0, q],
            recv_sem=core_sems.at[1, q],
            device_id=device(place, 1 - core),
            device_id_type=MESH,
        )

    for q in (xo, xp, xm, x):
        core_copy(q).start()

    row_index = []
    lane = lax.broadcasted_iota(I32, (GROUPS, ROWS), 1)
    for side in range(2):
        table = rows[:, side, :].astype(F32)
        for kk in range(4):
            hit = jnp.where(lane == virt * 4 + kk, table, 0.0)
            row_index.append(jnp.sum(hit, axis=1, keepdims=True).astype(I32))
    orbit = lax.broadcasted_iota(I32, (GROUPS, OCC), 1)
    hits = jnp.concatenate([(orbit == index).astype(F32) for index in row_index], axis=0)
    chosen = jnp.dot(hits, singles[...], precision=lax.Precision.HIGHEST, preferred_element_type=F32)
    chosen = jnp.concatenate([chosen, jnp.zeros((64, 64), F32)], axis=1)
    index_a = cols[:, 0, :]
    index_b = cols[:, 1, :]
    for kk in range(4):
        left = lookup(chosen[8 * kk : 8 * kk + 8], index_a)
        right = lookup(chosen[32 + 8 * kk : 40 + 8 * kk], index_b)
        value = t2_slab[:, kk, :] + left * right
        slab_send[:, kk, 0:128] = jnp.where(core == 0, value, 0.0)
        slab_send[:, 4 + kk, 0:128] = jnp.where(core == 0, 0.0, value)
        value = w_hole[:, kk, :]
        slab_send[:, kk, 128:384] = jnp.where(core == 0, value, 0.0)
        slab_send[:, 4 + kk, 128:384] = jnp.where(core == 0, 0.0, value)

    def h1_copy(d):
        to = lax.rem(z + d, NZ)
        return pltpu.make_async_remote_copy(
            src_ref=slab_send.at[to],
            dst_ref=slab_recv.at[z],
            send_sem=h1_sems.at[0, d],
            recv_sem=h1_sems.at[1, d],
            device_id=device(to * NY + y, core),
            device_id_type=MESH,
        )

    for d in range(1, NZ):
        h1_copy(d).start()
    slab_recv[z] = slab_send[z]

    def summed(q):
        core_copy(q).wait()
        mine[q] += got[q]

    def ring1_copy(way):
        lo = HALF * way
        return pltpu.make_async_remote_copy(
            src_ref=mine.at[xo, pl.ds(lo, HALF)],
            dst_ref=ring1.at[way],
            send_sem=ring_sems.at[0, way],
            recv_sem=ring_sems.at[1, way],
            device_id=(virt, xp if way == 0 else xm),
            device_id_type=MESH,
        )

    def ring2_copy(way, half):
        to = xp if way == 0 else xm
        return pltpu.make_async_remote_copy(
            src_ref=mine.at[to, pl.ds(HALF * half, HALF)],
            dst_ref=ring2.at[way, pl.ds(HALF * half, HALF)],
            send_sem=ring_sems.at[0, 2 + 2 * way + half],
            recv_sem=ring_sems.at[1, 2 + 2 * way + half],
            device_id=(virt, to),
            device_id_type=MESH,
        )

    summed(xo)
    ring1_copy(0).start()
    ring1_copy(1).start()
    summed(xp)
    ring2_copy(0, 1).start()
    summed(xm)
    ring2_copy(1, 0).start()

    def h2_copy(d):
        other = lax.rem(y * 2 + core + d, 2 * NY)
        return pltpu.make_async_remote_copy(
            src_ref=slab_recv.at[:, :, pl.ds(0, 128)],
            dst_ref=slab_all.at[core, :, y],
            send_sem=h2_sems.at[0, d],
            recv_sem=h2_sems.at[1, d],
            device_id=(z * 2 * NY + other, x),
            device_id_type=MESH,
        )

    for d in range(1, NZ):
        h1_copy(d).wait_recv()
    for d in range(1, 2 * NY):
        h2_copy(d).start()
    slab_all[core, :, y] = slab_recv[:, :, 0:128]

    ring1_copy(0).wait_recv()
    mine[xp, 0:HALF] += ring1[0]
    ring2_copy(0, 0).start()
    ring1_copy(1).wait_recv()
    mine[xm, HALF:PLACES] += ring1[1]
    ring2_copy(1, 1).start()
    summed(x)

    for d in range(1, 2 * NY):
        h2_copy(d).wait_recv()
    slab = (slab_all[0] + slab_all[1]).reshape(ROWS, 128)
    weights = slab_recv[:, :, 128:384].reshape(8 * NZ, ROWS)
    hole = jnp.dot(weights, slab, precision=lax.Precision.HIGHEST, preferred_element_type=F32)
    hole_send[...] = hole.reshape(NZ, 8, 128)

    def h3_copy(d):
        to = lax.rem(z + d, NZ)
        return pltpu.make_async_remote_copy(
            src_ref=hole_send.at[to],
            dst_ref=hole_recv.at[z],
            send_sem=h3_sems.at[0, d],
            recv_sem=h3_sems.at[1, d],
            device_id=device(to * NY + y, core),
            device_id_type=MESH,
        )

    for d in range(1, NZ):
        h3_copy(d).start()
    hole_recv[z] = hole_send[z]

    for way in range(2):
        for half in range(2):
            ring2_copy(way, half).wait_recv()
    mine[x] += ring2[0] + ring2[1]

    def all_copy(d):
        to = lax.rem(place + d, PLACES)
        return pltpu.make_async_remote_copy(
            src_ref=mine.at[x, to],
            dst_ref=recv.at[place],
            send_sem=all_sems.at[0, d],
            recv_sem=all_sems.at[1, d],
            device_id=device(to, core),
            device_id_type=MESH,
        )

    def all_start(d, carry):
        all_copy(d).start()
        return carry

    lax.fori_loop(1, PLACES, all_start, 0)
    recv[place] = mine[x, place]

    zeros = jnp.zeros((8, 64), F32)
    energy = jnp.concatenate([jnp.broadcast_to(vir[...], (8, VIRT)), zeros], axis=1)
    vir_sum = lookup(energy, index_a) + lookup(energy, index_b)
    occ_value = jnp.sum(hits * occ[...], axis=1, keepdims=True)
    column = lax.broadcasted_iota(I32, (32, PLACES * 8), 1)
    row = lax.broadcasted_iota(I32, (32, PLACES * 8), 0)
    position = (column >> 3) * PLACE + ((column >> 2) & 1) * (PLACE - 1)
    block = jnp.zeros_like(column)
    for h in range(1, GROUPS):
        block += (position >= starts[h]).astype(I32)
    pick = ((row & 7) == block) & ((row >> 3) == (column & 3))
    pick = pick.astype(F32)

    for d in range(1, NZ):
        h3_copy(d).wait_recv()

    def all_wait(d, carry):
        all_copy(d).wait()
        return carry

    lax.fori_loop(1, PLACES, all_wait, 0)
    ladder = jnp.dot(
        pick,
        recv[...].reshape(PLACES * 8, 128),
        precision=lax.Precision.HIGHEST,
        preferred_element_type=F32,
    )
    for kk in range(4):
        total = driver[:, kk, :] + ladder[8 * kk : 8 * kk + 8]
        total += hole_recv[:, kk, :] + hole_recv[:, 4 + kk, :]
        below = vir_sum - occ_value[8 * kk : 8 * kk + 8] - occ_value[32 + 8 * kk : 40 + 8 * kk]
        out[:, kk, :] = total / below

    for d in range(1, NZ):
        h1_copy(d).wait_send()
        h3_copy(d).wait_send()
        h2_copy(d).wait_send()
    for way in range(2):
        ring1_copy(way).wait_send()
        for half in range(2):
            ring2_copy(way, half).wait_send()


def body(
    t2_packed,
    w_packed,
    pair_list,
    block_starts,
    singles,
    row_pairs,
    col_pairs,
    t2_slab,
    w_hole,
    driver,
    occ_energy,
    vir_energy,
):
    vmem = pl.BlockSpec(memory_space=pltpu.VMEM)
    smem = pl.BlockSpec(memory_space=pltpu.SMEM)
    hbm = pl.BlockSpec(memory_space=pl.ANY)
    rows = row_pairs.transpose(0, 2, 1)
    cols = col_pairs.transpose(0, 2, 1)
    t2_steps = t2_packed.T.reshape(STEPS, STEP, ROWS)
    w_steps = w_packed.reshape(STEPS, STEP, COLS)
    part_a, part_b = pl.pallas_call(
        ladder_kernel,
        out_shape=[jax.ShapeDtypeStruct((ROWS, COLS), F32)] * 2,
        in_specs=[smem, vmem, vmem, vmem, hbm, hbm],
        out_specs=[vmem, vmem],
        scratch_shapes=[
            pltpu.VMEM((STEPS, STEP, ROWS), F32),
            pltpu.VMEM((STEPS, STEP, COLS), F32),
            pltpu.VMEM((STEPS, STEP, 8), I32),
            pltpu.VMEM((128, 1024), F32),
            pltpu.VMEM((1024, 256), BF16),
            pltpu.VMEM((2, 2, 256, ROWS), BF16),
            pltpu.SemaphoreType.DMA((2, STEPS)),
        ],
        compiler_params=pltpu.CompilerParams(vmem_limit_bytes=50 * 2**20),
        name="ladder",
    )(block_starts, singles, pair_list, rows, t2_steps, w_steps)
    tiles = (NX, PLACES, 8, 128)
    return pl.pallas_call(
        exchange_kernel,
        out_shape=jax.ShapeDtypeStruct((GROUPS, 4, 128), F32),
        in_specs=[smem] + [vmem] * 10,
        out_specs=vmem,
        scratch_shapes=[
            pltpu.VMEM(tiles, F32),
            pltpu.VMEM(tiles, F32),
            pltpu.VMEM(tiles, F32),
            pltpu.VMEM((2, HALF, 8, 128), F32),
            pltpu.VMEM((2, PLACES, 8, 128), F32),
            pltpu.VMEM((PLACES, 8, 128), F32),
            pltpu.VMEM((NZ, 8, 384), F32),
            pltpu.VMEM((NZ, 8, 384), F32),
            pltpu.VMEM((2, NZ, NY, 8, 128), F32),
            pltpu.VMEM((NZ, 8, 128), F32),
            pltpu.VMEM((NZ, 8, 128), F32),
            pltpu.SemaphoreType.DMA((2, NX)),
            pltpu.SemaphoreType.DMA((2, 6)),
            pltpu.SemaphoreType.DMA((2, PLACES)),
            pltpu.SemaphoreType.DMA((2, NZ)),
            pltpu.SemaphoreType.DMA((2, 2 * NY)),
            pltpu.SemaphoreType.DMA((2, NZ)),
        ],
        compiler_params=pltpu.CompilerParams(
            collective_id=0, has_side_effects=True, vmem_limit_bytes=40 * 2**20
        ),
        name="exchange",
    )(
        block_starts,
        part_a,
        part_b,
        singles,
        rows,
        cols,
        t2_slab,
        w_hole,
        driver,
        occ_energy.reshape(1, OCC),
        vir_energy.reshape(1, VIRT),
    )


def solution(mesh):
    in_specs = (
        P(None, ("virt", "rep")),
        P(("virt", "rep"), None),
        P(None, ("virt", "rep")),
        P(),
        P(),
        P(),
        P(None, "rep", None),
        P(None, "virt", "rep"),
        P(None, "virt", None),
        P(None, "virt", "rep"),
        P(),
        P(),
    )
    out_specs = P(None, "virt", "rep")
    return jax.shard_map(body, mesh=mesh, in_specs=in_specs, out_specs=out_specs, check_vma=False)
```

time: 421 us -> 50.9 us (0.12); the launches traced: 413 us -> 50.3 us
  waiting for transfers between devices: 239 us -> 0 us
  local copies, waits for them, and re-layouts: 122 us -> 3.81 us
  Pallas kernels: 0 us -> 46.4 us
  matrix products: 17.5 us -> 0 us
  between operations: 16.8 us -> 0.08 us
  loops' own time: 10.5 us -> 0 us
  other arithmetic: 6.88 us -> 0 us
    reduce_scatter x2 -> x0, waiting for transfers between devices: 142 us -> none  [the longest x1 142 us: body(): ladder = lax.psum_scatter(partly, 'virt', scatter_dimension=1, tiled=True)]
    gather x14 -> x0, local copies, waits for them, and re-layouts: 116 us -> none  [the longest x1 40.3 us: slab_dressing(): jnp.take_along_axis(left_rows, index_a, axis=2)]
    all_gather x1 -> x0, waiting for transfers between devices: 97.2 us -> none  [body(): lax.all_gather(slab_dressed, 'virt', axis=1, tiled=True)]
    pallas_call x0 -> x2, Pallas kernels: none -> 46.4 us  [the longest x1 31.3 us: body(): pl.pallas_call(exchange_kernel, out_shape=jax.ShapeDtypeStruct((GROUPS, 4...]
    dot_general x2 -> x0, matrix products: 17.5 us -> none  [the longest x1 14.9 us: single_block(): jnp.dot(t2_piece + terms, w_piece, precision=lax.Precision.HIGHEST, prefe...]
    another operation x1 -> x0, loops' own time: 10.5 us -> none  [ladder_pieces(): lax.cond(first_block == final_block, single_block, split_blocks, 0)]
  transfers between devices with their start and end apart: 3 -> 0, of which waited for: 2 -> 0; matrix products, arithmetic and copies ran while one was open for 23% -> 0% of each run, Pallas kernels for 0% -> 0%
where the time goes in v1:
time: 50.9 us; the launch traced here: 50.3 us
  Pallas kernels  46.4 us (91%)
  local copies, waits for them, and re-layouts  3.81 us (7%)
    pallas_call x1, Pallas kernels, body(): pl.pallas_call(exchange_kernel, out_shape=jax.ShapeDtypeStruct((GROUPS, 4...  31.3 us
    pallas_call x1, Pallas kernels, body(): pl.pallas_call(ladder_kernel, out_shape=[jax.ShapeDtypeStruct((ROWS, COLS...  15.1 us
    unnamed x21, local copies, waits for them, and re-layouts  3.81 us

profile of v1, /device:TPU:2, one launch (start us, length us, event | category | flops | bytes accessed | tf_op | source)
XLA Modules:
  0.0 50.3 jit_solution(14401289361040855399)
XLA Ops:
  0.0 0.0 copy-start.9
  0.0 0.0 copy-start.6
  0.0 0.0 copy-start
  0.0 1.1 %copy-done = f32[120,960]{1,0:T(8,128)S(1)} copy-done((f32[120,960]{1,0:T(8,128)S(1)}, f32[120,960]{1,0:T(8,128)}, u32[]{:S(2)}) %copy-start) | copy-done | bytes 460824
  1.1 0.0 copy-start.1
  1.1 0.7 %copy-done.1 = s32[8,256,2]{1,2,0:T(2,128)S(1)} copy-done((s32[8,256,2]{1,2,0:T(2,128)S(1)}, s32[8,256,2]{1,2,0:T(2,128)}, u32[]{:S(2)}) %copy-start.1) | copy-done | bytes 16408
  1.8 0.0 copy-start.3
  1.8 0.7 %copy-done.3 = s32[2,3600]{1,0:T(2,128)S(1)} copy-done((s32[2,3600]{1,0:T(2,128)S(1)}, s32[2,3600]{1,0:T(2,128)}, u32[]{:S(2)}) %copy-start.3) | copy-done | bytes 28824
  2.5 0.0 copy-start.8
  2.5 0.7 %copy-done.8 = s32[8]{0:T(128)S(1)} copy-done((s32[8]{0:T(128)S(1)}, s32[8]{0:T(128)}, u32[]{:S(2)}) %copy-start.8) | copy-done | bytes 56
  3.2 0.0 copy-start.2
  3.2 0.0 copy-start.4
  3.2 0.0 copy-start.5
  3.2 0.0 copy-start.7
  3.2 15.1 %ladder.1 = (f32[256,512]{1,0:T(8,128)S(1)}, f32[256,512]{1,0:T(8,128)S(1)}) custom-call(s32[8]{0:T(128)S(1)} %copy-done.8, f32[120,960]{1,0:T(8,128)S(1)} %copy-done, s32[2,3600]{1,0:T(2,128)S(1)} %copy-done.3, s32[8,2,256]{2,1,0:T(2,128)S(1)} %bitcast.8, f32[5,720,256]{2,1,0:T(8,128)} %bitcast.14, f32[5,720,512]{2,1,0:T(8,128)} %bitcast.13), custom_call_target="tpu_custom_call" | custom-call | tf_op jit(solution)/shard_map/ladder/pallas_call | solution.py:427
  18.4 0.0 copy-done.9
  18.4 0.0 copy-done.6
  18.4 0.0 copy-done.2
  18.4 0.0 copy-done.4
  18.4 0.0 copy-done.5
  18.4 0.0 copy-done.7
  18.4 31.3 %exchange.1 = f32[8,4,128]{2,1,0:T(4,128)S(1)} custom-call(s32[8]{0:T(128)S(1)} %copy-done.8, f32[256,512]{1,0:T(8,128)S(1)} %get-tuple-element.7.part_a, f32[256,512]{1,0:T(8,128)S(1)} %get-tuple-element.8.part_b, f32[120,960]{1,0:T(8,128)S(1)} %copy-done, s32[8,2,256]{2,1,0:T(2,128)S(1)} %bitcast.9, s32[8,2,128]{2,1,0:T(2,128)S(1)} %bitcast.10, ...), custom_call_target="tpu_custom_call" | custom-call | tf_op jit(solution)/shard_map/exchange/pallas_call | solution.py:445
  49.7 0.6 %copy.14 = f32[8,4,128]{2,1,0:T(4,128)} copy(f32[8,4,128]{2,1,0:T(4,128)S(1)} %exchange.1) | data formatting | bytes 32768
Async XLA Ops:
  0.0 18.4 %copy-start.9 = (f32[120]{0:T(128)S(1)}, f32[120]{0:T(128)}, u32[]{:S(2)}) copy-start(f32[120]{0:T(128)} %param.22) | copy-start | bytes 1444
  0.0 18.4 %copy-start.6 = (s32[8,128,2]{1,2,0:T(2,128)S(1)}, s32[8,128,2]{1,2,0:T(2,128)}, u32[]{:S(2)}) copy-start(s32[8,128,2]{1,2,0:T(2,128)} %param.18) | copy-start | bytes 24580
  0.0 1.1 %copy-start = (f32[120,960]{1,0:T(8,128)S(1)}, f32[120,960]{1,0:T(8,128)}, u32[]{:S(2)}) copy-start(f32[120,960]{1,0:T(8,128)} %singles.3) | copy-start | bytes 1382404
  1.1 0.7 %copy-start.1 = (s32[8,256,2]{1,2,0:T(2,128)S(1)}, s32[8,256,2]{1,2,0:T(2,128)}, u32[]{:S(2)}) copy-start(s32[8,256,2]{1,2,0:T(2,128)} %param.17) | copy-start | bytes 49156
  1.8 0.8 %copy-start.3 = (s32[2,3600]{1,0:T(2,128)S(1)}, s32[2,3600]{1,0:T(2,128)}, u32[]{:S(2)}) copy-start(s32[2,3600]{1,0:T(2,128)} %pairs.1) | copy-start | bytes 86404
  2.5 0.7 %copy-start.8 = (s32[8]{0:T(128)S(1)}, s32[8]{0:T(128)}, u32[]{:S(2)}) copy-start(s32[8]{0:T(128)} %starts.3) | copy-start | bytes 100
  3.2 15.2 %copy-start.2 = (f32[8,4,256]{2,1,0:T(4,128)S(1)}, f32[8,4,256]{2,1,0:T(4,128)}, u32[]{:S(2)}) copy-start(f32[8,4,256]{2,1,0:T(4,128)} %w_hole.1) | copy-start | bytes 98308
  3.2 15.2 %copy-start.4 = (f32[8,4,128]{2,1,0:T(4,128)S(1)}, f32[8,4,128]{2,1,0:T(4,128)}, u32[]{:S(2)}) copy-start(f32[8,4,128]{2,1,0:T(4,128)} %t2_slab.1) | copy-start | bytes 49156
  3.2 15.2 %copy-start.5 = (f32[8,4,128]{2,1,0:T(4,128)S(1)}, f32[8,4,128]{2,1,0:T(4,128)}, u32[]{:S(2)}) copy-start(f32[8,4,128]{2,1,0:T(4,128)} %driver.1) | copy-start | bytes 49156
  3.2 15.2 %copy-start.7 = (f32[960]{0:T(1024)S(1)}, f32[960]{0:T(1024)}, u32[]{:S(2)}) copy-start(f32[960]{0:T(1024)} %param.23) | copy-start | bytes 11524

commit v2 on v1

v2 whole, which is shorter than its diff:
```python
import jax
import jax.numpy as jnp
from jax import lax
from jax.experimental import pallas as pl
from jax.experimental.pallas import tpu as pltpu
from jax.sharding import PartitionSpec as P

MESH = pl.DeviceIdType.MESH
F32 = jnp.float32
BF16 = jnp.bfloat16
I32 = jnp.int32

GROUPS = 8
OCC = 120
VIRT = 960
ROWS = 256
COLS = 512
PIECE = 3600
STEP = 240
STEPS = PIECE // STEP
JOIN = 3
CHUNK = STEP * JOIN
CHUNKS = STEPS // JOIN
NZ = 8
NY = 4
NX = 4
PLACES = NZ * NY
PLACE = 8 * PIECE
PARTS = 4
PART = PLACES // PARTS
HALF = PART // 2


def split(value):
    high = value.astype(BF16)
    return high, (value - high.astype(F32)).astype(BF16)


def block_at(starts, position):
    block = jnp.int32(0)
    for h in range(1, GROUPS):
        block += (position >= starts[h]).astype(I32)
    return block


def over_rows(left, right):
    return lax.dot_general(left, right, (((0,), (0,)), ((), ())), preferred_element_type=F32)


def lookup(columns, index):
    low = index & 127
    tile = index >> 7
    found = jnp.zeros((8, 128), F32)
    for t in range(8):
        piece = jnp.take_along_axis(
            columns[:, 128 * t : 128 * (t + 1)], low, axis=1, mode="promise_in_bounds"
        )
        found = jnp.where(tile == t, piece, found)
    return found


def ladder_kernel(
    starts_hbm,
    singles_hbm,
    pairs_hbm,
    rows_hbm,
    cols_hbm,
    slab_hbm,
    hole_hbm,
    driver_hbm,
    occ_hbm,
    vir_hbm,
    t2_hbm,
    w_hbm,
    out,
    starts,
    singles,
    pairs,
    rows,
    cols,
    t2_slab,
    w_hole,
    driver,
    occ,
    vir,
    t2,
    w,
    pair,
    padded,
    table,
    select,
    sum_a,
    sum_b,
    mine,
    give,
    got,
    ring1,
    ring2,
    recv,
    slab_send,
    slab_recv,
    slab_all,
    hole_send,
    hole_recv,
    small_sems,
    load_sems,
    core_sems,
    ring_sems,
    all_sems,
    h1_sems,
    h2_sems,
    h3_sems,
):
    virt = lax.axis_index("virt")
    x = lax.axis_index("rep")
    core = lax.rem(virt, 2)
    place = virt // 2
    y = lax.rem(place, NY)
    z = place // NY
    xp = lax.rem(x + 1, NX)
    xo = lax.rem(x + 2, NX)
    xm = lax.rem(x + 3, NX)

    small = [
        pltpu.make_async_copy(source, target, small_sems.at[n])
        for n, (source, target) in enumerate(
            (
                (starts_hbm, starts),
                (singles_hbm, singles),
                (pairs_hbm, pairs),
                (rows_hbm, rows),
                (cols_hbm, cols),
                (slab_hbm, t2_slab),
                (hole_hbm, w_hole),
                (driver_hbm, driver),
                (occ_hbm, occ),
                (vir_hbm, vir),
            )
        )
    ]
    for copy in small:
        copy.start()

    def load(k):
        piece = pl.ds(k * JOIN, JOIN)
        return (
            pltpu.make_async_copy(t2_hbm.at[piece], t2.at[piece], load_sems.at[0, k]),
            pltpu.make_async_copy(w_hbm.at[piece], w.at[piece], load_sems.at[1, k]),
        )

    for k in range(CHUNKS):
        for copy in load(k):
            copy.start()

    def device(place_to, core_to):
        return (place_to * 2 + core_to, x)

    barrier = pltpu.get_barrier_semaphore()

    def greet(target):
        pl.semaphore_signal(barrier, inc=1, device_id=target, device_id_type=MESH)

    greet(device(place, 1 - core))
    greet((virt, xp))
    greet((virt, xm))

    def greet_place(d, carry):
        greet(device(lax.rem(place + d, PLACES), core))
        return carry

    lax.fori_loop(1, PLACES, greet_place, 0)
    for d in range(1, NY):
        greet(device(z * NY + lax.rem(y + d, NY), 1 - core))

    for copy in small:
        copy.wait()

    segment = virt * NX + x
    block_a = block_at(starts, place * PLACE)
    block_b = block_at(starts, place * PLACE + PLACE - 1)
    count = jnp.clip(starts[block_b] - segment * PIECE, 0, PIECE)
    mixed = jnp.minimum(count // STEP, STEPS - 1)
    padded[...] = jnp.zeros_like(padded)
    padded[0:OCC, 0:VIRT] = singles[...]
    high, low = split(padded[...].T)
    table[:, 0:128] = high
    table[:, 128:256] = low
    for k in range(STEPS):
        part = pairs[:, k * STEP : (k + 1) * STEP]
        pair[k] = jnp.concatenate([part, jnp.zeros((6, STEP), I32)], axis=0).T
    orbit = lax.broadcasted_iota(I32, (128, ROWS), 0)
    for s, block in enumerate((block_a, block_b)):
        for side in range(2):
            hit = (orbit == rows[block, side : side + 1, :]).astype(F32)
            select[s, side] = jnp.concatenate([hit, hit], axis=0).astype(BF16)
    sum_a[...] = jnp.zeros_like(sum_a)
    sum_b[...] = jnp.zeros_like(sum_b)

    row_index = []
    lane = lax.broadcasted_iota(I32, (GROUPS, ROWS), 1)
    for side in range(2):
        both = rows[:, side, :].astype(F32)
        for kk in range(4):
            hit = jnp.where(lane == virt * 4 + kk, both, 0.0)
            row_index.append(jnp.sum(hit, axis=1, keepdims=True).astype(I32))
    orbit = lax.broadcasted_iota(I32, (GROUPS, OCC), 1)
    hits = jnp.concatenate([(orbit == index).astype(F32) for index in row_index], axis=0)
    chosen = jnp.dot(hits, singles[...], precision=lax.Precision.HIGHEST, preferred_element_type=F32)
    chosen = jnp.concatenate([chosen, jnp.zeros((64, 64), F32)], axis=1)
    index_a = cols[:, 0, :]
    index_b = cols[:, 1, :]
    for kk in range(4):
        left = lookup(chosen[8 * kk : 8 * kk + 8], index_a)
        right = lookup(chosen[32 + 8 * kk : 40 + 8 * kk], index_b)
        value = t2_slab[:, kk, :] + left * right
        slab_send[:, kk, 0:128] = jnp.where(core == 0, value, 0.0)
        slab_send[:, 4 + kk, 0:128] = jnp.where(core == 0, 0.0, value)
        value = w_hole[:, kk, :]
        slab_send[:, kk, 128:384] = jnp.where(core == 0, value, 0.0)
        slab_send[:, 4 + kk, 128:384] = jnp.where(core == 0, 0.0, value)

    def gathered(index):
        hit = (lax.broadcasted_iota(I32, (index.shape[0], 1024), 1) == index).astype(BF16)
        return jnp.dot(hit, table[...], preferred_element_type=F32).astype(BF16)

    def dressed(k, orbit_c, orbit_d, select_i, select_j):
        left = jnp.dot(orbit_c, select_i, preferred_element_type=F32)
        right = jnp.dot(orbit_d, select_j, preferred_element_type=F32)
        return t2[k] + left * right

    def product(value, k):
        value_high, value_low = split(value)
        w_high, w_low = split(w[k])
        return (
            over_rows(value_high, w_high) + over_rows(value_high, w_low) + over_rows(value_low, w_high)
        )

    def chunk(k):
        for copy in load(k):
            copy.wait()
        index = pair[pl.ds(k * JOIN, JOIN)].reshape(CHUNK, 8)
        orbit_c = gathered(index[:, 0:1])
        orbit_d = gathered(index[:, 1:2])
        for s in range(JOIN):
            step = k * JOIN + s
            piece = slice(s * STEP, (s + 1) * STEP)
            in_a = step < mixed
            value = dressed(
                step,
                orbit_c[piece],
                orbit_d[piece],
                jnp.where(in_a, select[0, 0], select[1, 0]),
                jnp.where(in_a, select[0, 1], select[1, 1]),
            )
            part = product(value, step)
            sum_a[...] += part * jnp.where(step < mixed, 1.0, 0.0)
            sum_b[...] += part * jnp.where(step > mixed, 1.0, 0.0)

    def h1_copy(d):
        to = lax.rem(z + d, NZ)
        return pltpu.make_async_remote_copy(
            src_ref=slab_send.at[to],
            dst_ref=slab_recv.at[z],
            send_sem=h1_sems.at[0, d],
            recv_sem=h1_sems.at[1, d],
            device_id=device(to * NY + y, core),
            device_id_type=MESH,
        )

    def h2_copy(d):
        other = lax.rem(y * 2 + core + d, 2 * NY)
        return pltpu.make_async_remote_copy(
            src_ref=slab_recv.at[:, :, pl.ds(0, 128)],
            dst_ref=slab_all.at[core, :, y],
            send_sem=h2_sems.at[0, d],
            recv_sem=h2_sems.at[1, d],
            device_id=(z * 2 * NY + other, x),
            device_id_type=MESH,
        )

    def h3_copy(d):
        to = lax.rem(z + d, NZ)
        return pltpu.make_async_remote_copy(
            src_ref=hole_send.at[to],
            dst_ref=hole_recv.at[z],
            send_sem=h3_sems.at[0, d],
            recv_sem=h3_sems.at[1, d],
            device_id=device(to * NY + y, core),
            device_id_type=MESH,
        )

    chunk(0)
    pl.semaphore_wait(barrier, 2 + PLACES - 1 + 1 + NY - 1)
    for d in range(1, NZ):
        h1_copy(d).start()
    slab_recv[z] = slab_send[z]
    chunk(1)
    for d in range(1, NZ):
        h1_copy(d).wait_recv()
    for d in range(1, 2 * NY):
        h2_copy(d).start()
    slab_all[core, :, y] = slab_recv[:, :, 0:128]
    chunk(2)
    chunk(3)
    for d in range(1, 2 * NY):
        h2_copy(d).wait_recv()
    slab = (slab_all[0] + slab_all[1]).reshape(ROWS, 128)
    weights = slab_recv[:, :, 128:384].reshape(8 * NZ, ROWS)
    hole = jnp.dot(weights, slab, precision=lax.Precision.HIGHEST, preferred_element_type=F32)
    hole_send[...] = hole.reshape(NZ, 8, 128)
    for d in range(1, NZ):
        h3_copy(d).start()
    hole_recv[z] = hole_send[z]
    chunk(4)

    index = pair[mixed]
    orbit_c = gathered(index[:, 0:1])
    orbit_d = gathered(index[:, 1:2])
    mask = lax.broadcasted_iota(I32, (STEP, ROWS), 0) < count - mixed * STEP
    value_a = jnp.where(mask, dressed(mixed, orbit_c, orbit_d, select[0, 0], select[0, 1]), 0.0)
    sum_a[...] += product(value_a, mixed)
    value_b = jnp.where(mask, 0.0, dressed(mixed, orbit_c, orbit_d, select[1, 0], select[1, 1]))
    sum_b[...] += product(value_b, mixed)

    def first(g):
        return lax.rem(z // 2 + 1 + g, PARTS) * PART

    def core_copy(g):
        tiles = pl.ds(first(g), PART)
        return pltpu.make_async_remote_copy(
            src_ref=give.at[:, tiles],
            dst_ref=got.at[:, tiles],
            send_sem=core_sems.at[0, g],
            recv_sem=core_sems.at[1, g],
            device_id=device(place, 1 - core),
            device_id_type=MESH,
        )

    def ring1_copy(g, way):
        return pltpu.make_async_remote_copy(
            src_ref=mine.at[xo, pl.ds(first(g) + HALF * way, HALF)],
            dst_ref=ring1.at[way, g],
            send_sem=ring_sems.at[0, g, way],
            recv_sem=ring_sems.at[1, g, way],
            device_id=(virt, xp if way == 0 else xm),
            device_id_type=MESH,
        )

    def ring2_copy(g, way, half):
        to = xp if way == 0 else xm
        tiles = pl.ds(first(g) + HALF * half, HALF)
        return pltpu.make_async_remote_copy(
            src_ref=mine.at[to, tiles],
            dst_ref=ring2.at[way, tiles],
            send_sem=ring_sems.at[0, g, 2 + 2 * way + half],
            recv_sem=ring_sems.at[1, g, 2 + 2 * way + half],
            device_id=(virt, to),
            device_id_type=MESH,
        )

    def all_copy(d):
        to = lax.rem(place + d, PLACES)
        return pltpu.make_async_remote_copy(
            src_ref=mine.at[x, to],
            dst_ref=recv.at[place],
            send_sem=all_sems.at[0, d],
            recv_sem=all_sems.at[1, d],
            device_id=device(to, core),
            device_id_type=MESH,
        )

    upper = lax.broadcasted_iota(I32, (PART, 8, 128), 1) < 4
    for g in range(PARTS):
        rows_of = pl.ds(pl.multiple_of(first(g) * 8, 8 * PART), 8 * PART)
        tiles = pl.ds(first(g), PART)
        for q in range(NX):
            a = sum_a[rows_of, 128 * q : 128 * (q + 1)].reshape(PART, 8, 128)
            b = sum_b[rows_of, 128 * q : 128 * (q + 1)].reshape(PART, 8, 128)
            tile0 = jnp.where(upper, a, pltpu.roll(b, 4, 1))
            tile1 = jnp.where(upper, pltpu.roll(a, 4, 1), b)
            mine[q, tiles] = jnp.where(core == 0, tile0, tile1)
            give[q, tiles] = jnp.where(core == 0, tile1, tile0)
        core_copy(g).start()

    zeros = jnp.zeros((8, 64), F32)
    energy = jnp.concatenate([jnp.broadcast_to(vir[...], (8, VIRT)), zeros], axis=1)
    vir_sum = lookup(energy, index_a) + lookup(energy, index_b)
    occ_value = jnp.sum(hits * occ[...], axis=1, keepdims=True)
    column = lax.broadcasted_iota(I32, (32, PLACES * 8), 1)
    row = lax.broadcasted_iota(I32, (32, PLACES * 8), 0)
    position = (column >> 3) * PLACE + ((column >> 2) & 1) * (PLACE - 1)
    block = jnp.zeros_like(column)
    for h in range(1, GROUPS):
        block += (position >= starts[h]).astype(I32)
    pick = ((row & 7) == block) & ((row >> 3) == (column & 3))
    pick = pick.astype(F32)

    for g in range(PARTS):
        tiles = pl.ds(first(g), PART)
        core_copy(g).wait()
        mine[:, tiles] += got[:, tiles]
        for way in range(2):
            ring1_copy(g, way).start()
        ring2_copy(g, 0, 1).start()
        ring2_copy(g, 1, 0).start()
    for g in range(PARTS):
        for way, to in ((0, xp), (1, xm)):
            tiles = pl.ds(first(g) + HALF * way, HALF)
            ring1_copy(g, way).wait_recv()
            mine[to, tiles] += ring1[way, g]
            ring2_copy(g, way, way).start()
    for g in range(PARTS):
        tiles = pl.ds(first(g), PART)
        for way in range(2):
            for half in range(2):
                ring2_copy(g, way, half).wait_recv()
        mine[x, tiles] += ring2[0, tiles] + ring2[1, tiles]

        def all_start(n, carry):
            d = lax.rem(first(g) + n - place + PLACES, PLACES)

            @pl.when(d > 0)
            def _():
                all_copy(d).start()

            return carry

        lax.fori_loop(0, PART, all_start, 0)
    recv[place] = mine[x, place]

    for d in range(1, NZ):
        h3_copy(d).wait_recv()

    def all_wait(d, carry):
        all_copy(d).wait()
        return carry

    lax.fori_loop(1, PLACES, all_wait, 0)
    ladder = jnp.dot(
        pick,
        recv[...].reshape(PLACES * 8, 128),
        precision=lax.Precision.HIGHEST,
        preferred_element_type=F32,
    )
    for kk in range(4):
        total = driver[:, kk, :] + ladder[8 * kk : 8 * kk + 8]
        total += hole_recv[:, kk, :] + hole_recv[:, 4 + kk, :]
        below = vir_sum - occ_value[8 * kk : 8 * kk + 8] - occ_value[32 + 8 * kk : 40 + 8 * kk]
        out[:, kk, :] = total / below

    for d in range(1, NZ):
        h1_copy(d).wait_send()
        h3_copy(d).wait_send()
        h2_copy(d).wait_send()
    for g in range(PARTS):
        for way in range(2):
            ring1_copy(g, way).wait_send()
            for half in range(2):
                ring2_copy(g, way, half).wait_send()


def body(
    t2_packed,
    w_packed,
    pair_list,
    block_starts,
    singles,
    row_pairs,
    col_pairs,
    t2_slab,
    w_hole,
    driver,
    occ_energy,
    vir_energy,
):
    hbm = pl.BlockSpec(memory_space=pl.ANY)
    tiles = (NX, PLACES, 8, 128)
    return pl.pallas_call(
        ladder_kernel,
        out_shape=jax.ShapeDtypeStruct((GROUPS, 4, 128), F32),
        in_specs=[hbm] * 12,
        out_specs=pl.BlockSpec(memory_space=pltpu.VMEM),
        scratch_shapes=[
            pltpu.SMEM((GROUPS,), I32),
            pltpu.VMEM((OCC, VIRT), F32),
            pltpu.VMEM((2, PIECE), I32),
            pltpu.VMEM((GROUPS, 2, ROWS), I32),
            pltpu.VMEM((GROUPS, 2, 128), I32),
            pltpu.VMEM((GROUPS, 4, 128), F32),
            pltpu.VMEM((GROUPS, 4, ROWS), F32),
            pltpu.VMEM((GROUPS, 4, 128), F32),
            pltpu.VMEM((1, OCC), F32),
            pltpu.VMEM((1, VIRT), F32),
            pltpu.VMEM((STEPS, STEP, ROWS), F32),
            pltpu.VMEM((STEPS, STEP, COLS), F32),
            pltpu.VMEM((STEPS, STEP, 8), I32),
            pltpu.VMEM((128, 1024), F32),
            pltpu.VMEM((1024, 256), BF16),
            pltpu.VMEM((2, 2, 256, ROWS), BF16),
            pltpu.VMEM((ROWS, COLS), F32),
            pltpu.VMEM((ROWS, COLS), F32),
            pltpu.VMEM(tiles, F32),
            pltpu.VMEM(tiles, F32),
            pltpu.VMEM(tiles, F32),
            pltpu.VMEM((2, PARTS, HALF, 8, 128), F32),
            pltpu.VMEM((2, PLACES, 8, 128), F32),
            pltpu.VMEM((PLACES, 8, 128), F32),
            pltpu.VMEM((NZ, 8, 384), F32),
            pltpu.VMEM((NZ, 8, 384), F32),
            pltpu.VMEM((2, NZ, NY, 8, 128), F32),
            pltpu.VMEM((NZ, 8, 128), F32),
            pltpu.VMEM((NZ, 8, 128), F32),
            pltpu.SemaphoreType.DMA((10,)),
            pltpu.SemaphoreType.DMA((2, CHUNKS)),
            pltpu.SemaphoreType.DMA((2, PARTS)),
            pltpu.SemaphoreType.DMA((2, PARTS, 6)),
            pltpu.SemaphoreType.DMA((2, PLACES)),
            pltpu.SemaphoreType.DMA((2, NZ)),
            pltpu.SemaphoreType.DMA((2, 2 * NY)),
            pltpu.SemaphoreType.DMA((2, NZ)),
        ],
        compiler_params=pltpu.CompilerParams(
            collective_id=0, has_side_effects=True, vmem_limit_bytes=60 * 2**20
        ),
        name="ladder",
    )(
        block_starts,
        singles,
        pair_list,
        row_pairs.transpose(0, 2, 1),
        col_pairs.transpose(0, 2, 1),
        t2_slab,
        w_hole,
        driver,
        occ_energy.reshape(1, OCC),
        vir_energy.reshape(1, VIRT),
        t2_packed.T.reshape(STEPS, STEP, ROWS),
        w_packed.reshape(STEPS, STEP, COLS),
    )


def solution(mesh):
    in_specs = (
        P(None, ("virt", "rep")),
        P(("virt", "rep"), None),
        P(None, ("virt", "rep")),
        P(),
        P(),
        P(),
        P(None, "rep", None),
        P(None, "virt", "rep"),
        P(None, "virt", None),
        P(None, "virt", "rep"),
        P(),
        P(),
    )
    out_specs = P(None, "virt", "rep")
    return jax.shard_map(body, mesh=mesh, in_specs=in_specs, out_specs=out_specs, check_vma=False)
```

time: 50.9 us -> 45.3 us (0.89)
  Pallas kernels: 46.4 us -> 43.6 us
  local copies, waits for them, and re-layouts: 3.81 us -> 1.32 us
    pallas_call x2 -> x1, Pallas kernels: 46.4 us -> 43.6 us  [body(): pl.pallas_call(ladder_kernel, out_shape=jax.ShapeDtypeStruct((GROUPS, 4,...]
    unnamed x21 -> x1, local copies, waits for them, and re-layouts: 3.81 us -> 1.32 us
where the time goes in v2:
time: 45.3 us; the launch traced here: 45 us
  Pallas kernels  43.6 us (96%)
  local copies, waits for them, and re-layouts  1.32 us (3%)
    pallas_call x1, Pallas kernels, body(): pl.pallas_call(ladder_kernel, out_shape=jax.ShapeDtypeStruct((GROUPS, 4,...  43.6 us
    unnamed x1, local copies, waits for them, and re-layouts  1.32 us

profile of v2, /device:TPU:2, one launch (start us, length us, event | category | flops | bytes accessed | tf_op | source)
XLA Modules:
  0.0 45.0 jit_solution(594795154926764129)
XLA Ops:
  0.0 43.6 %ladder.1 = f32[8,4,128]{2,1,0:T(4,128)} custom-call(s32[8]{0:T(128)} %starts_hbm.1, f32[120,960]{1,0:T(8,128)} %singles_hbm.1, s32[2,3600]{1,0:T(2,128)} %pairs_hbm.1, s32[8,2,256]{2,1,0:T(2,128)} %bitcast.10, s32[8,2,128]{2,1,0:T(2,128)} %bitcast.11, f32[8,4,128]{2,1,0:T(4,128)} %slab_hbm.1, f32[8,4,256]{2,1,0:T(4,128)} %hole_hbm.1, ...), custom_call_target="tpu_custom_call" | custom-call | tf_op jit(solution)/shard_map/ladder/pallas_call | solution.py:478
  43.7 1.3 %copy.14 = f32[8,4,128]{2,1,0:T(4,128)} copy(f32[8,4,128]{2,1,0:T(4,128)} %ladder.1) | data formatting | bytes 32768

commit v3 on v2

v3 whole, which is shorter than its diff:
```python
import jax
import jax.numpy as jnp
from jax import lax
from jax.experimental import pallas as pl
from jax.experimental.pallas import tpu as pltpu
from jax.sharding import PartitionSpec as P

MESH = pl.DeviceIdType.MESH
F32 = jnp.float32
BF16 = jnp.bfloat16
I32 = jnp.int32

GROUPS = 8
OCC = 120
VIRT = 960
ROWS = 256
COLS = 512
PIECE = 3600
CHUNK = 720
CHUNKS = PIECE // CHUNK
WIDE = COLS // 2
NZ = 8
NY = 4
NX = 4
PLACES = NZ * NY
PLACE = 8 * PIECE
PARTS = 4
PART = PLACES // PARTS
HALF = PLACES // 2


def split(value):
    high = value.astype(BF16)
    return high, (value - high.astype(F32)).astype(BF16)


def block_at(starts, position):
    block = jnp.int32(0)
    for h in range(1, GROUPS):
        block += (position >= starts[h]).astype(I32)
    return block


def over_rows(left, right):
    return lax.dot_general(left, right, (((0,), (0,)), ((), ())), preferred_element_type=F32)


def lookup(columns, index):
    low = index & 127
    tile = index >> 7
    found = jnp.zeros((8, 128), F32)
    for t in range(8):
        piece = jnp.take_along_axis(
            columns[:, 128 * t : 128 * (t + 1)], low, axis=1, mode="promise_in_bounds"
        )
        found = jnp.where(tile == t, piece, found)
    return found


def ladder_kernel(
    starts_hbm,
    singles_hbm,
    pairs_hbm,
    rows_hbm,
    cols_hbm,
    slab_hbm,
    hole_hbm,
    driver_hbm,
    occ_hbm,
    vir_hbm,
    t2_hbm,
    w_hbm,
    out,
    starts,
    singles,
    pairs,
    rows,
    cols,
    t2_slab,
    w_hole,
    driver,
    occ,
    vir,
    t2,
    w,
    pair,
    padded,
    table,
    select,
    sum_a,
    sum_b,
    mine,
    give,
    got,
    ring1,
    ring2,
    recv,
    orbits,
    d_high,
    d_low,
    slab_send,
    slab_recv,
    slab_all,
    hole_send,
    hole_recv,
    small_sems,
    load_sems,
    core_sems,
    ring_sems,
    late_sems,
    all_sems,
    hole_sems,
):
    virt = lax.axis_index("virt")
    x = lax.axis_index("rep")
    core = lax.rem(virt, 2)
    place = virt // 2
    y = lax.rem(place, NY)
    z = place // NY
    xp = lax.rem(x + 1, NX)
    xo = lax.rem(x + 2, NX)
    xm = lax.rem(x + 3, NX)

    small = [
        pltpu.make_async_copy(source, target, small_sems.at[n])
        for n, (source, target) in enumerate(
            (
                (starts_hbm, starts),
                (singles_hbm, singles),
                (pairs_hbm, pairs),
                (rows_hbm, rows),
                (cols_hbm, cols),
                (slab_hbm, t2_slab),
                (hole_hbm, w_hole),
                (driver_hbm, driver),
                (occ_hbm, occ),
                (vir_hbm, vir),
            )
        )
    ]
    for copy in small:
        copy.start()

    def load_t2(k):
        return pltpu.make_async_copy(t2_hbm.at[k], t2.at[k], load_sems.at[0, k])

    def load_w(k):
        return pltpu.make_async_copy(w_hbm.at[k], w.at[k], load_sems.at[1, k])

    load_t2(0).start()
    load_t2(1).start()

    def device(place_to, core_to):
        return (place_to * 2 + core_to, x)

    barrier = pltpu.get_barrier_semaphore()

    def greet(target):
        pl.semaphore_signal(barrier, inc=1, device_id=target, device_id_type=MESH)

    greet(device(place, 1 - core))
    greet((virt, xp))
    greet((virt, xm))

    for d in range(1, PLACES):
        greet(device(lax.rem(place + d, PLACES), core))
    for d in range(1, NY):
        greet(device(z * NY + lax.rem(y + d, NY), 1 - core))

    for copy in small:
        copy.wait()

    segment = virt * NX + x
    block_a = block_at(starts, place * PLACE)
    block_b = block_at(starts, place * PLACE + PLACE - 1)
    count = jnp.clip(starts[block_b] - segment * PIECE, 0, PIECE)
    mixed = jnp.minimum(count // CHUNK, CHUNKS - 1)
    padded[...] = jnp.zeros_like(padded)
    padded[0:OCC, 0:VIRT] = singles[...]
    high, low = split(padded[...].T)
    table[:, 0:128] = high
    table[:, 128:256] = low
    for k in range(CHUNKS):
        part = pairs[:, k * CHUNK : (k + 1) * CHUNK]
        pair[k] = jnp.concatenate([part, jnp.zeros((6, CHUNK), I32)], axis=0).T
    orbit = lax.broadcasted_iota(I32, (128, ROWS), 0)
    for s, block in enumerate((block_a, block_b)):
        for side in range(2):
            hit = (orbit == rows[block, side : side + 1, :]).astype(F32)
            select[s, side] = jnp.concatenate([hit, hit], axis=0).astype(BF16)

    row_index = []
    lane = lax.broadcasted_iota(I32, (GROUPS, ROWS), 1)
    for side in range(2):
        both = rows[:, side, :].astype(F32)
        for kk in range(4):
            hit = jnp.where(lane == virt * 4 + kk, both, 0.0)
            row_index.append(jnp.sum(hit, axis=1, keepdims=True).astype(I32))
    orbit = lax.broadcasted_iota(I32, (GROUPS, OCC), 1)
    hits = jnp.concatenate([(orbit == index).astype(F32) for index in row_index], axis=0)
    chosen = jnp.dot(hits, singles[...], precision=lax.Precision.HIGHEST, preferred_element_type=F32)
    chosen = jnp.concatenate([chosen, jnp.zeros((64, 64), F32)], axis=1)
    index_a = cols[:, 0, :]
    index_b = cols[:, 1, :]
    for kk in range(4):
        left = lookup(chosen[8 * kk : 8 * kk + 8], index_a)
        right = lookup(chosen[32 + 8 * kk : 40 + 8 * kk], index_b)
        value = t2_slab[:, kk, :] + left * right
        slab_send[:, kk, 0:128] = jnp.where(core == 0, value, 0.0)
        slab_send[:, 4 + kk, 0:128] = jnp.where(core == 0, 0.0, value)
        value = w_hole[:, kk, :]
        slab_send[:, kk, 128:384] = jnp.where(core == 0, value, 0.0)
        slab_send[:, 4 + kk, 128:384] = jnp.where(core == 0, 0.0, value)

    def gathered(index):
        hit = (lax.broadcasted_iota(I32, (index.shape[0], 1024), 1) == index).astype(BF16)
        return jnp.dot(hit, table[...], preferred_element_type=F32).astype(BF16)

    def dressed(k, select_i, select_j):
        left = jnp.dot(orbits[0, k], select_i, preferred_element_type=F32)
        right = jnp.dot(orbits[1, k], select_j, preferred_element_type=F32)
        return t2[k] + left * right

    in_chunk = lax.broadcasted_iota(I32, (CHUNK, ROWS), 0)

    def dress(k):
        if k + 2 < CHUNKS:
            load_t2(k + 2).start()
        load_w(k).start()
        load_t2(k).wait()
        index = pair[k]
        orbits[0, k] = gathered(index[:, 0:1])
        orbits[1, k] = gathered(index[:, 1:2])
        in_a = k <= mixed
        value = dressed(
            k,
            jnp.where(in_a, select[0, 0], select[1, 0]),
            jnp.where(in_a, select[0, 1], select[1, 1]),
        )
        bound = jnp.where(k > mixed, CHUNK, count - k * CHUNK)
        d_high[k], d_low[k] = split(jnp.where(in_chunk < bound, value, 0.0))

    def dress_rest():
        value = dressed(mixed, select[1, 0], select[1, 1])
        value = jnp.where(in_chunk < count - mixed * CHUNK, 0.0, value)
        d_high[CHUNKS], d_low[CHUNKS] = split(value)

    def product(k, n, half):
        columns = pl.ds(pl.multiple_of(half * WIDE, WIDE), WIDE)
        w_high, w_low = split(w[n, :, columns])
        return (
            over_rows(d_high[k], w_high) + over_rows(d_high[k], w_low) + over_rows(d_low[k], w_high)
        )

    def multiply(k, half):
        part = product(k, k, half)
        sum_a[...] += part * jnp.where(k <= mixed, 1.0, 0.0)
        sum_b[...] += part * jnp.where(k > mixed, 1.0, 0.0)

    def h1_copy(d):
        to = lax.rem(z + d, NZ)
        return pltpu.make_async_remote_copy(
            src_ref=slab_send.at[to],
            dst_ref=slab_recv.at[z],
            send_sem=hole_sems.at[0, 0],
            recv_sem=hole_sems.at[1, 0],
            device_id=device(to * NY + y, core),
            device_id_type=MESH,
        )

    def h2_copy(d):
        other = lax.rem(y * 2 + core + d, 2 * NY)
        return pltpu.make_async_remote_copy(
            src_ref=slab_recv.at[:, :, pl.ds(0, 128)],
            dst_ref=slab_all.at[core, :, y],
            send_sem=hole_sems.at[0, 1],
            recv_sem=hole_sems.at[1, 1],
            device_id=(z * 2 * NY + other, x),
            device_id_type=MESH,
        )

    def h3_copy(d):
        to = lax.rem(z + d, NZ)
        return pltpu.make_async_remote_copy(
            src_ref=hole_send.at[to],
            dst_ref=hole_recv.at[z],
            send_sem=hole_sems.at[0, 2],
            recv_sem=hole_sems.at[1, 2],
            device_id=device(to * NY + y, core),
            device_id_type=MESH,
        )

    def wait_bytes(ref, sem):
        pltpu.make_async_copy(ref, ref, sem).wait()

    def h1_wait(end):
        wait_bytes(slab_recv.at[pl.ds(0, NZ - 1)], hole_sems.at[end, 0])

    def h2_wait(end):
        wait_bytes(slab_all.at[:, pl.ds(0, NZ - 1)], hole_sems.at[end, 1])

    def h3_wait(end):
        wait_bytes(hole_recv.at[pl.ds(0, NZ - 1)], hole_sems.at[end, 2])

    own = x // 2
    far = 1 - own
    odd = lax.rem(x, 2)
    way_far = 1 - odd
    way_own = odd
    to_far = jnp.where(odd == 0, xm, xp)
    to_own = jnp.where(odd == 0, xp, xm)

    def first(g):
        return lax.rem(z // 2 + 1 + g, PARTS) * PART

    def core_copy(half, tiles, n):
        part = (pl.ds(2 * half, 2), tiles)
        return pltpu.make_async_remote_copy(
            src_ref=give.at[part],
            dst_ref=got.at[part],
            send_sem=core_sems.at[0, n],
            recv_sem=core_sems.at[1, n],
            device_id=device(place, 1 - core),
            device_id_type=MESH,
        )

    def ring1_copy(way):
        return pltpu.make_async_remote_copy(
            src_ref=mine.at[xo, pl.ds(HALF * way, HALF)],
            dst_ref=ring1.at[way],
            send_sem=ring_sems.at[0, 0],
            recv_sem=ring_sems.at[1, 1 + way],
            device_id=(virt, xp if way == 0 else xm),
            device_id_type=MESH,
        )

    def ring2_copy(way, to, tiles, recv_sem):
        return pltpu.make_async_remote_copy(
            src_ref=mine.at[to, tiles],
            dst_ref=ring2.at[way, tiles],
            send_sem=ring_sems.at[0, 0],
            recv_sem=recv_sem,
            device_id=(virt, to),
            device_id_type=MESH,
        )

    def all_copy(to):
        return pltpu.make_async_remote_copy(
            src_ref=mine.at[x, to],
            dst_ref=recv.at[place],
            send_sem=all_sems.at[0],
            recv_sem=all_sems.at[1],
            device_id=device(to, core),
            device_id_type=MESH,
        )

    upper = lax.broadcasted_iota(I32, (PART, 8, 128), 1) < 4

    def assemble(half, g):
        rows_of = pl.ds(pl.multiple_of(first(g) * 8, 8 * PART), 8 * PART)
        tiles = pl.ds(first(g), PART)
        for j in range(2):
            a = sum_a[rows_of, 128 * j : 128 * (j + 1)].reshape(PART, 8, 128)
            b = sum_b[rows_of, 128 * j : 128 * (j + 1)].reshape(PART, 8, 128)
            tile0 = jnp.where(upper, a, pltpu.roll(b, 4, 1))
            tile1 = jnp.where(upper, pltpu.roll(a, 4, 1), b)
            mine[2 * half + j, tiles] = jnp.where(core == 0, tile0, tile1)
            give[2 * half + j, tiles] = jnp.where(core == 0, tile1, tile0)

    everything = pl.ds(0, PLACES)

    for k in range(CHUNKS):
        dress(k)
    dress_rest()
    pl.semaphore_wait(barrier, 2 + PLACES - 1 + 1 + NY - 1)
    for d in range(1, NZ):
        h1_copy(d).start()
    slab_recv[z] = slab_send[z]

    sum_a[...] = jnp.zeros_like(sum_a)
    sum_b[...] = jnp.zeros_like(sum_b)
    for k in range(CHUNKS):
        load_w(k).wait()
        multiply(k, far)
    sum_b[...] += product(CHUNKS, mixed, far)
    for g in range(PARTS):
        assemble(far, g)
    core_copy(far, everything, 0).start()

    h1_wait(1)
    for d in range(1, 2 * NY):
        h2_copy(d).start()
    slab_all[core, :, y] = slab_recv[:, :, 0:128]

    sum_a[...] = jnp.zeros_like(sum_a)
    sum_b[...] = jnp.zeros_like(sum_b)
    multiply(0, own)
    multiply(1, own)
    core_copy(far, everything, 0).wait()
    for j in range(2):
        mine[2 * far + j] += got[2 * far + j]
    for way in range(2):
        ring1_copy(way).start()
    ring2_copy(way_far, to_far, pl.ds(HALF * (1 - way_far), HALF), ring_sems.at[1, 0]).start()
    multiply(2, own)
    multiply(3, own)
    multiply(4, own)
    sum_b[...] += product(CHUNKS, mixed, own)
    for g in range(PARTS):
        assemble(own, g)
        core_copy(own, pl.ds(first(g), PART), 1 + g).start()

    zeros = jnp.zeros((8, 64), F32)
    energy = jnp.concatenate([jnp.broadcast_to(vir[...], (8, VIRT)), zeros], axis=1)
    vir_sum = lookup(energy, index_a) + lookup(energy, index_b)
    occ_value = jnp.sum(hits * occ[...], axis=1, keepdims=True)
    column = lax.broadcasted_iota(I32, (32, PLACES * 8), 1)
    row = lax.broadcasted_iota(I32, (32, PLACES * 8), 0)
    position = (column >> 3) * PLACE + ((column >> 2) & 1) * (PLACE - 1)
    block = jnp.zeros_like(column)
    for h in range(1, GROUPS):
        block += (position >= starts[h]).astype(I32)
    pick = ((row & 7) == block) & ((row >> 3) == (column & 3))
    pick = pick.astype(F32)

    h2_wait(1)
    slab = (slab_all[0] + slab_all[1]).reshape(ROWS, 128)
    weights = slab_recv[:, :, 128:384].reshape(8 * NZ, ROWS)
    hole = jnp.dot(weights, slab, precision=lax.Precision.HIGHEST, preferred_element_type=F32)
    hole_send[...] = hole.reshape(NZ, 8, 128)
    for d in range(1, NZ):
        h3_copy(d).start()
    hole_recv[z] = hole_send[z]

    for way in range(2):
        wait_bytes(ring1.at[way], ring_sems.at[1, 1 + way])
    half_far = pl.ds(HALF * way_far, HALF)
    mine[to_far, half_far] += ring1[way_far]
    ring2_copy(way_far, to_far, half_far, ring_sems.at[1, 0]).start()
    mine[to_own, pl.ds(HALF * way_own, HALF)] += ring1[way_own]

    for g in range(PARTS):
        tiles = pl.ds(first(g), PART)
        core_copy(own, tiles, 1 + g).wait()
        for j in range(2):
            mine[2 * own + j, tiles] += got[2 * own + j, tiles]
        ring2_copy(way_own, to_own, tiles, late_sems.at[g]).start()
    wait_bytes(ring2.at[0], ring_sems.at[1, 0])
    for g in range(PARTS):
        tiles = pl.ds(first(g), PART)
        wait_bytes(ring2.at[0, tiles], late_sems.at[g])
        mine[x, tiles] += ring2[0, tiles] + ring2[1, tiles]

        for n in range(1 if g == PARTS - 1 else 0, PART):
            if g == PARTS - 1:
                to = first(g) + lax.rem(place - first(g) + n, PART)
            else:
                to = first(g) + n
            all_copy(to).start()
    recv[place] = mine[x, place]

    h3_wait(1)
    wait_bytes(recv.at[pl.ds(0, PLACES - 1)], all_sems.at[1])
    ladder = jnp.dot(
        pick,
        recv[...].reshape(PLACES * 8, 128),
        precision=lax.Precision.HIGHEST,
        preferred_element_type=F32,
    )
    for kk in range(4):
        total = driver[:, kk, :] + ladder[8 * kk : 8 * kk + 8]
        total += hole_recv[:, kk, :] + hole_recv[:, 4 + kk, :]
        below = vir_sum - occ_value[8 * kk : 8 * kk + 8] - occ_value[32 + 8 * kk : 40 + 8 * kk]
        out[:, kk, :] = total / below

    h1_wait(0)
    h2_wait(0)
    h3_wait(0)
    wait_bytes(recv.at[pl.ds(0, PLACES - 1)], all_sems.at[0])
    wait_bytes(mine.at[pl.ds(0, NX - 1)], ring_sems.at[0, 0])


def body(
    t2_packed,
    w_packed,
    pair_list,
    block_starts,
    singles,
    row_pairs,
    col_pairs,
    t2_slab,
    w_hole,
    driver,
    occ_energy,
    vir_energy,
):
    hbm = pl.BlockSpec(memory_space=pl.ANY)
    tiles = (NX, PLACES, 8, 128)
    return pl.pallas_call(
        ladder_kernel,
        out_shape=jax.ShapeDtypeStruct((GROUPS, 4, 128), F32),
        in_specs=[hbm] * 12,
        out_specs=pl.BlockSpec(memory_space=pltpu.VMEM),
        scratch_shapes=[
            pltpu.SMEM((GROUPS,), I32),
            pltpu.VMEM((OCC, VIRT), F32),
            pltpu.VMEM((2, PIECE), I32),
            pltpu.VMEM((GROUPS, 2, ROWS), I32),
            pltpu.VMEM((GROUPS, 2, 128), I32),
            pltpu.VMEM((GROUPS, 4, 128), F32),
            pltpu.VMEM((GROUPS, 4, ROWS), F32),
            pltpu.VMEM((GROUPS, 4, 128), F32),
            pltpu.VMEM((1, OCC), F32),
            pltpu.VMEM((1, VIRT), F32),
            pltpu.VMEM((CHUNKS, CHUNK, ROWS), F32),
            pltpu.VMEM((CHUNKS, CHUNK, COLS), F32),
            pltpu.VMEM((CHUNKS, CHUNK, 8), I32),
            pltpu.VMEM((128, 1024), F32),
            pltpu.VMEM((1024, 256), BF16),
            pltpu.VMEM((2, 2, 256, ROWS), BF16),
            pltpu.VMEM((ROWS, WIDE), F32),
            pltpu.VMEM((ROWS, WIDE), F32),
            pltpu.VMEM(tiles, F32),
            pltpu.VMEM(tiles, F32),
            pltpu.VMEM(tiles, F32),
            pltpu.VMEM((2, HALF, 8, 128), F32),
            pltpu.VMEM((2, PLACES, 8, 128), F32),
            pltpu.VMEM((PLACES, 8, 128), F32),
            pltpu.VMEM((2, CHUNKS, CHUNK, 256), BF16),
            pltpu.VMEM((CHUNKS + 1, CHUNK, ROWS), BF16),
            pltpu.VMEM((CHUNKS + 1, CHUNK, ROWS), BF16),
            pltpu.VMEM((NZ, 8, 384), F32),
            pltpu.VMEM((NZ, 8, 384), F32),
            pltpu.VMEM((2, NZ, NY, 8, 128), F32),
            pltpu.VMEM((NZ, 8, 128), F32),
            pltpu.VMEM((NZ, 8, 128), F32),
            pltpu.SemaphoreType.DMA((10,)),
            pltpu.SemaphoreType.DMA((2, CHUNKS)),
            pltpu.SemaphoreType.DMA((2, 1 + PARTS)),
            pltpu.SemaphoreType.DMA((2, 3)),
            pltpu.SemaphoreType.DMA((PARTS,)),
            pltpu.SemaphoreType.DMA((2,)),
            pltpu.SemaphoreType.DMA((2, 3)),
        ],
        compiler_params=pltpu.CompilerParams(
            collective_id=0, has_side_effects=True, vmem_limit_bytes=60 * 2**20
        ),
        name="ladder",
    )(
        block_starts,
        singles,
        pair_list,
        row_pairs.transpose(0, 2, 1),
        col_pairs.transpose(0, 2, 1),
        t2_slab,
        w_hole,
        driver,
        occ_energy.reshape(1, OCC),
        vir_energy.reshape(1, VIRT),
        t2_packed.T.reshape(CHUNKS, CHUNK, ROWS),
        w_packed.reshape(CHUNKS, CHUNK, COLS),
    )


def solution(mesh):
    in_specs = (
        P(None, ("virt", "rep")),
        P(("virt", "rep"), None),
        P(None, ("virt", "rep")),
        P(),
        P(),
        P(),
        P(None, "rep", None),
        P(None, "virt", "rep"),
        P(None, "virt", None),
        P(None, "virt", "rep"),
        P(),
        P(),
    )
    out_specs = P(None, "virt", "rep")
    return jax.shard_map(body, mesh=mesh, in_specs=in_specs, out_specs=out_specs, check_vma=False)
```

time: 45.3 us -> 37.8 us (0.83)
  Pallas kernels: 43.6 us -> 35.8 us
    pallas_call x1, Pallas kernels: 43.6 us -> 35.8 us  [body(): pl.pallas_call(ladder_kernel, out_shape=jax.ShapeDtypeStruct((GROUPS, 4,...]
where the time goes in v3:
time: 37.8 us; the launch traced here: 37.1 us
  Pallas kernels  35.8 us (95%)
  local copies, waits for them, and re-layouts  1.32 us (3%)
    pallas_call x1, Pallas kernels, body(): pl.pallas_call(ladder_kernel, out_shape=jax.ShapeDtypeStruct((GROUPS, 4,...  35.8 us
    unnamed x1, local copies, waits for them, and re-layouts  1.32 us

profile of v3, /device:TPU:2, one launch (start us, length us, event | category | flops | bytes accessed | tf_op | source)
XLA Modules:
  0.0 37.1 jit_solution(16232368089103946232)
XLA Ops:
  0.0 35.8 %ladder.1 = f32[8,4,128]{2,1,0:T(4,128)} custom-call(s32[8]{0:T(128)} %starts_hbm.1, f32[120,960]{1,0:T(8,128)} %singles_hbm.1, s32[2,3600]{1,0:T(2,128)} %pairs_hbm.1, s32[8,2,256]{2,1,0:T(2,128)} %bitcast.10, s32[8,2,128]{2,1,0:T(2,128)} %bitcast.11, f32[8,4,128]{2,1,0:T(4,128)} %slab_hbm.1, f32[8,4,256]{2,1,0:T(4,128)} %hole_hbm.1, ...), custom_call_target="tpu_custom_call" | custom-call | tf_op jit(solution)/shard_map/ladder/pallas_call | solution.py:499
  35.8 1.3 %copy.14 = f32[8,4,128]{2,1,0:T(4,128)} copy(f32[8,4,128]{2,1,0:T(4,128)} %ladder.1) | data formatting | bytes 32768

commit v4 on v3

--- a/solution.py
+++ b/solution.py
@@ -87,8 +87,7 @@
     padded,
     table,
     select,
-    sum_a,
-    sum_b,
+    parts,
     mine,
     give,
     got,
@@ -253,9 +252,16 @@
         )
 
     def multiply(k, half):
-        part = product(k, k, half)
-        sum_a[...] += part * jnp.where(k <= mixed, 1.0, 0.0)
-        sum_b[...] += part * jnp.where(k > mixed, 1.0, 0.0)
+        parts[k] = product(k, k, half)
+
+    def sums(rows_of, columns):
+        a = jnp.zeros((8 * PART, 128), F32)
+        b = parts[CHUNKS, rows_of, columns]
+        for k in range(CHUNKS):
+            part = parts[k, rows_of, columns]
+            a += part * jnp.where(k <= mixed, 1.0, 0.0)
+            b += part * jnp.where(k > mixed, 1.0, 0.0)
+        return a.reshape(PART, 8, 128), b.reshape(PART, 8, 128)
 
     def h1_copy(d):
         to = lax.rem(z + d, NZ)
@@ -360,8 +366,7 @@
         rows_of = pl.ds(pl.multiple_of(first(g) * 8, 8 * PART), 8 * PART)
         tiles = pl.ds(first(g), PART)
         for j in range(2):
-            a = sum_a[rows_of, 128 * j : 128 * (j + 1)].reshape(PART, 8, 128)
-            b = sum_b[rows_of, 128 * j : 128 * (j + 1)].reshape(PART, 8, 128)
+            a, b = sums(rows_of, slice(128 * j, 128 * (j + 1)))
             tile0 = jnp.where(upper, a, pltpu.roll(b, 4, 1))
             tile1 = jnp.where(upper, pltpu.roll(a, 4, 1), b)
             mine[2 * half + j, tiles] = jnp.where(core == 0, tile0, tile1)
@@ -377,12 +382,11 @@
         h1_copy(d).start()
     slab_recv[z] = slab_send[z]
 
-    sum_a[...] = jnp.zeros_like(sum_a)
-    sum_b[...] = jnp.zeros_like(sum_b)
     for k in range(CHUNKS):
         load_w(k).wait()
+    for k in range(CHUNKS):
         multiply(k, far)
-    sum_b[...] += product(CHUNKS, mixed, far)
+    parts[CHUNKS] = product(CHUNKS, mixed, far)
     for g in range(PARTS):
         assemble(far, g)
     core_copy(far, everything, 0).start()
@@ -392,8 +396,6 @@
         h2_copy(d).start()
     slab_all[core, :, y] = slab_recv[:, :, 0:128]
 
-    sum_a[...] = jnp.zeros_like(sum_a)
-    sum_b[...] = jnp.zeros_like(sum_b)
     multiply(0, own)
     multiply(1, own)
     core_copy(far, everything, 0).wait()
@@ -405,10 +407,46 @@
     multiply(2, own)
     multiply(3, own)
     multiply(4, own)
-    sum_b[...] += product(CHUNKS, mixed, own)
+    parts[CHUNKS] = product(CHUNKS, mixed, own)
     for g in range(PARTS):
         assemble(own, g)
         core_copy(own, pl.ds(first(g), PART), 1 + g).start()
+
+    for way in range(2):
+        wait_bytes(ring1.at[way], ring_sems.at[1, 1 + way])
+    half_far = pl.ds(HALF * way_far, HALF)
+    mine[to_far, half_far] += ring1[way_far]
+    ring2_copy(way_far, to_far, half_far, ring_sems.at[1, 0]).start()
+    mine[to_own, pl.ds(HALF * way_own, HALF)] += ring1[way_own]
+
+    for g in range(PARTS):
+        tiles = pl.ds(first(g), PART)
+        core_copy(own, tiles, 1 + g).wait()
+        for j in range(2):
+            mine[2 * own + j, tiles] += got[2 * own + j, tiles]
+        ring2_copy(way_own, to_own, tiles, late_sems.at[g]).start()
+    h2_wait(1)
+    slab = (slab_all[0] + slab_all[1]).reshape(ROWS, 128)
+    weights = slab_recv[:, :, 128:384].reshape(8 * NZ, ROWS)
+    hole = jnp.dot(weights, slab, precision=lax.Precision.HIGHEST, preferred_element_type=F32)
+    hole_send[...] = hole.reshape(NZ, 8, 128)
+    for d in range(1, NZ):
+        h3_copy(d).start()
+    hole_recv[z] = hole_send[z]
+
+    wait_bytes(ring2.at[0], ring_sems.at[1, 0])
+    for g in range(PARTS):
+        tiles = pl.ds(first(g), PART)
+        wait_bytes(ring2.at[0, tiles], late_sems.at[g])
+        mine[x, tiles] += ring2[0, tiles] + ring2[1, tiles]
+
+        for n in range(1 if g == PARTS - 1 else 0, PART):
+            if g == PARTS - 1:
+                to = first(g) + lax.rem(place - first(g) + n, PART)
+            else:
+                to = first(g) + n
+            all_copy(to).start()
+    recv[place] = mine[x, place]
 
     zeros = jnp.zeros((8, 64), F32)
     energy = jnp.concatenate([jnp.broadcast_to(vir[...], (8, VIRT)), zeros], axis=1)
@@ -421,52 +459,17 @@
     for h in range(1, GROUPS):
         block += (position >= starts[h]).astype(I32)
     pick = ((row & 7) == block) & ((row >> 3) == (column & 3))
-    pick = pick.astype(F32)
-
-    h2_wait(1)
-    slab = (slab_all[0] + slab_all[1]).reshape(ROWS, 128)
-    weights = slab_recv[:, :, 128:384].reshape(8 * NZ, ROWS)
-    hole = jnp.dot(weights, slab, precision=lax.Precision.HIGHEST, preferred_element_type=F32)
-    hole_send[...] = hole.reshape(NZ, 8, 128)
-    for d in range(1, NZ):
-        h3_copy(d).start()
-    hole_recv[z] = hole_send[z]
-
-    for way in range(2):
-        wait_bytes(ring1.at[way], ring_sems.at[1, 1 + way])
-    half_far = pl.ds(HALF * way_far, HALF)
-    mine[to_far, half_far] += ring1[way_far]
-    ring2_copy(way_far, to_far, half_far, ring_sems.at[1, 0]).start()
-    mine[to_own, pl.ds(HALF * way_own, HALF)] += ring1[way_own]
-
-    for g in range(PARTS):
-        tiles = pl.ds(first(g), PART)
-        core_copy(own, tiles, 1 + g).wait()
-        for j in range(2):
-            mine[2 * own + j, tiles] += got[2 * own + j, tiles]
-        ring2_copy(way_own, to_own, tiles, late_sems.at[g]).start()
-    wait_bytes(ring2.at[0], ring_sems.at[1, 0])
-    for g in range(PARTS):
-        tiles = pl.ds(first(g), PART)
-        wait_bytes(ring2.at[0, tiles], late_sems.at[g])
-        mine[x, tiles] += ring2[0, tiles] + ring2[1, tiles]
-
-        for n in range(1 if g == PARTS - 1 else 0, PART):
-            if g == PARTS - 1:
-                to = first(g) + lax.rem(place - first(g) + n, PART)
-            else:
-                to = first(g) + n
-            all_copy(to).start()
-    recv[place] = mine[x, place]
+    pick = pick.astype(F32).astype(BF16)
 
     h3_wait(1)
     wait_bytes(recv.at[pl.ds(0, PLACES - 1)], all_sems.at[1])
-    ladder = jnp.dot(
-        pick,
-        recv[...].reshape(PLACES * 8, 128),
-        precision=lax.Precision.HIGHEST,
-        preferred_element_type=F32,
-    )
+    tiles = recv[...].reshape(PLACES * 8, 128)
+    high = tiles.astype(BF16)
+    rest = tiles - high.astype(F32)
+    middle, low = split(rest)
+    ladder = jnp.dot(pick, low, preferred_element_type=F32)
+    ladder += jnp.dot(pick, middle, preferred_element_type=F32)
+    ladder += jnp.dot(pick, high, preferred_element_type=F32)
     for kk in range(4):
         total = driver[:, kk, :] + ladder[8 * kk : 8 * kk + 8]
         total += hole_recv[:, kk, :] + hole_recv[:, 4 + kk, :]
@@ -498,7 +501,7 @@
     tiles = (NX, PLACES, 8, 128)
     return pl.pallas_call(
         ladder_kernel,
-        out_shape=jax.ShapeDtypeStruct((GROUPS, 4, 128), F32),
+        out_shape=pltpu.VMEM((GROUPS, 4, 128), F32),
         in_specs=[hbm] * 12,
         out_specs=pl.BlockSpec(memory_space=pltpu.VMEM),
         scratch_shapes=[
@@ -518,8 +521,7 @@
             pltpu.VMEM((128, 1024), F32),
             pltpu.VMEM((1024, 256), BF16),
             pltpu.VMEM((2, 2, 256, ROWS), BF16),
-            pltpu.VMEM((ROWS, WIDE), F32),
-            pltpu.VMEM((ROWS, WIDE), F32),
+            pltpu.VMEM((CHUNKS + 1, ROWS, WIDE), F32),
             pltpu.VMEM(tiles, F32),
             pltpu.VMEM(tiles, F32),
             pltpu.VMEM(tiles, F32),

time: 37.8 us -> 34.9 us (0.923); the launches traced: 37.1 us -> 34.8 us
  Pallas kernels: 35.8 us -> 34.2 us
  local copies, waits for them, and re-layouts: 1.32 us -> 0.61 us
    pallas_call x1, Pallas kernels: 35.8 us -> 34.2 us  [body(): pl.pallas_call(ladder_kernel, out_shape=pltpu.VMEM((GROUPS, 4, 128), F32)...]
    unnamed x1, local copies, waits for them, and re-layouts: 1.32 us -> 0.61 us
where the time goes in v4:
time: 34.9 us; the launch traced here: 34.8 us
  Pallas kernels  34.2 us (98%)
  local copies, waits for them, and re-layouts  0.61 us (2%)
    pallas_call x1, Pallas kernels, body(): pl.pallas_call(ladder_kernel, out_shape=pltpu.VMEM((GROUPS, 4, 128), F32)...  34.2 us

profile of v4, /device:TPU:2, one launch (start us, length us, event | category | flops | bytes accessed | tf_op | source)
XLA Modules:
  0.0 34.8 jit_solution(14001973479722181392)
XLA Ops:
  0.0 34.2 %ladder.1 = f32[8,4,128]{2,1,0:T(4,128)S(1)} custom-call(s32[8]{0:T(128)} %starts_hbm.1, f32[120,960]{1,0:T(8,128)} %singles_hbm.1, s32[2,3600]{1,0:T(2,128)} %pairs_hbm.1, s32[8,2,256]{2,1,0:T(2,128)} %bitcast.10, s32[8,2,128]{2,1,0:T(2,128)} %bitcast.11, f32[8,4,128]{2,1,0:T(4,128)} %slab_hbm.1, f32[8,4,256]{2,1,0:T(4,128)} %hole_hbm.1, ...), custom_call_target="tpu_custom_call" | custom-call | tf_op jit(solution)/shard_map/ladder/pallas_call | solution.py:502
  34.2 0.6 %copy.14 = f32[8,4,128]{2,1,0:T(4,128)} copy(f32[8,4,128]{2,1,0:T(4,128)S(1)} %ladder.1) | data formatting | bytes 32768

commit v5 on v4

--- a/solution.py
+++ b/solution.py
@@ -137,7 +137,7 @@
             )
         )
     ]
-    for copy in small:
+    for copy in small[:4]:
         copy.start()
 
     def load_t2(k):
@@ -147,6 +147,8 @@
         return pltpu.make_async_copy(w_hbm.at[k], w.at[k], load_sems.at[1, k])
 
     load_t2(0).start()
+    for copy in small[4:]:
+        copy.start()
     load_t2(1).start()
 
     def device(place_to, core_to):
@@ -166,7 +168,7 @@
     for d in range(1, NY):
         greet(device(z * NY + lax.rem(y + d, NY), 1 - core))
 
-    for copy in small:
+    for copy in small[:4]:
         copy.wait()
 
     segment = virt * NX + x
@@ -187,6 +189,176 @@
         for side in range(2):
             hit = (orbit == rows[block, side : side + 1, :]).astype(F32)
             select[s, side] = jnp.concatenate([hit, hit], axis=0).astype(BF16)
+
+    def gathered(index):
+        hit = (lax.broadcasted_iota(I32, (index.shape[0], 1024), 1) == index).astype(BF16)
+        return jnp.dot(hit, table[...], preferred_element_type=F32).astype(BF16)
+
+    def dressed(k, select_i, select_j):
+        left = jnp.dot(orbits[0, k], select_i, preferred_element_type=F32)
+        right = jnp.dot(orbits[1, k], select_j, preferred_element_type=F32)
+        return t2[k] + left * right
+
+    in_chunk = lax.broadcasted_iota(I32, (CHUNK, ROWS), 0)
+
+    def dress(k):
+        if k + 2 < CHUNKS:
+            load_t2(k + 2).start()
+        load_w(k).start()
+        load_t2(k).wait()
+        index = pair[k]
+        orbits[0, k] = gathered(index[:, 0:1])
+        orbits[1, k] = gathered(index[:, 1:2])
+        in_a = k <= mixed
+        value = dressed(
+            k,
+            jnp.where(in_a, select[0, 0], select[1, 0]),
+            jnp.where(in_a, select[0, 1], select[1, 1]),
+        )
+        bound = jnp.where(k > mixed, CHUNK, count - k * CHUNK)
+        d_high[k], d_low[k] = split(jnp.where(in_chunk < bound, value, 0.0))
+
+    def dress_rest():
+        value = dressed(mixed, select[1, 0], select[1, 1])
+        value = jnp.where(in_chunk < count - mixed * CHUNK, 0.0, value)
+        d_high[CHUNKS], d_low[CHUNKS] = split(value)
+
+    def product(k, n, half):
+        columns = pl.ds(pl.multiple_of(half * WIDE, WIDE), WIDE)
+        w_high, w_low = split(w[n, :, columns])
+        return (
+            over_rows(d_high[k], w_high) + over_rows(d_high[k], w_low) + over_rows(d_low[k], w_high)
+        )
+
+    def multiply(k, half):
+        parts[k] = product(k, k, half)
+
+    def sums(rows_of, columns):
+        a = jnp.zeros((8 * PART, 128), F32)
+        b = parts[CHUNKS, rows_of, columns]
+        for k in range(CHUNKS):
+            part = parts[k, rows_of, columns]
+            a += part * jnp.where(k <= mixed, 1.0, 0.0)
+            b += part * jnp.where(k > mixed, 1.0, 0.0)
+        return a.reshape(PART, 8, 128), b.reshape(PART, 8, 128)
+
+    def h1_copy(d):
+        to = lax.rem(z + d, NZ)
+        return pltpu.make_async_remote_copy(
+            src_ref=slab_send.at[to],
+            dst_ref=slab_recv.at[z],
+            send_sem=hole_sems.at[0, 0],
+            recv_sem=hole_sems.at[1, 0],
+            device_id=device(to * NY + y, core),
+            device_id_type=MESH,
+        )
+
+    def h2_copy(d):
+        other = lax.rem(y * 2 + core + d, 2 * NY)
+        return pltpu.make_async_remote_copy(
+            src_ref=slab_recv.at[:, :, pl.ds(0, 128)],
+            dst_ref=slab_all.at[core, :, y],
+            send_sem=hole_sems.at[0, 1],
+            recv_sem=hole_sems.at[1, 1],
+            device_id=(z * 2 * NY + other, x),
+            device_id_type=MESH,
+        )
+
+    def h3_copy(d):
+        to = lax.rem(z + d, NZ)
+        return pltpu.make_async_remote_copy(
+            src_ref=hole_send.at[to],
+            dst_ref=hole_recv.at[z],
+            send_sem=hole_sems.at[0, 2],
+            recv_sem=hole_sems.at[1, 2],
+            device_id=device(to * NY + y, core),
+            device_id_type=MESH,
+        )
+
+    def wait_bytes(ref, sem):
+        pltpu.make_async_copy(ref, ref, sem).wait()
+
+    def h1_wait(end):
+        wait_bytes(slab_recv.at[pl.ds(0, NZ - 1)], hole_sems.at[end, 0])
+
+    def h2_wait(end):
+        wait_bytes(slab_all.at[:, pl.ds(0, NZ - 1)], hole_sems.at[end, 1])
+
+    def h3_wait(end):
+        wait_bytes(hole_recv.at[pl.ds(0, NZ - 1)], hole_sems.at[end, 2])
+
+    own = x // 2
+    far = 1 - own
+    odd = lax.rem(x, 2)
+    way_far = 1 - odd
+    way_own = odd
+    to_far = jnp.where(odd == 0, xm, xp)
+    to_own = jnp.where(odd == 0, xp, xm)
+
+    def first(g):
+        return lax.rem(z // 2 + 1 + g, PARTS) * PART
+
+    def core_copy(half, tiles, n):
+        part = (pl.ds(2 * half, 2), tiles)
+        return pltpu.make_async_remote_copy(
+            src_ref=give.at[part],
+            dst_ref=got.at[part],
+            send_sem=core_sems.at[0, n],
+            recv_sem=core_sems.at[1, n],
+            device_id=device(place, 1 - core),
+            device_id_type=MESH,
+        )
+
+    def ring1_copy(way):
+        return pltpu.make_async_remote_copy(
+            src_ref=mine.at[xo, pl.ds(HALF * way, HALF)],
+            dst_ref=ring1.at[way],
+            send_sem=ring_sems.at[0, 0],
+            recv_sem=ring_sems.at[1, 1 + way],
+            device_id=(virt, xp if way == 0 else xm),
+            device_id_type=MESH,
+        )
+
+    def ring2_copy(way, to, tiles, recv_sem):
+        return pltpu.make_async_remote_copy(
+            src_ref=mine.at[to, tiles],
+            dst_ref=ring2.at[way, tiles],
+            send_sem=ring_sems.at[0, 0],
+            recv_sem=recv_sem,
+            device_id=(virt, to),
+            device_id_type=MESH,
+        )
+
+    def all_copy(to):
+        return pltpu.make_async_remote_copy(
+            src_ref=mine.at[x, to],
+            dst_ref=recv.at[place],
+            send_sem=all_sems.at[0],
+            recv_sem=all_sems.at[1],
+            device_id=device(to, core),
+            device_id_type=MESH,
+        )
+
+    upper = lax.broadcasted_iota(I32, (PART, 8, 128), 1) < 4
+
+    def assemble(half, g):
+        rows_of = pl.ds(pl.multiple_of(first(g) * 8, 8 * PART), 8 * PART)
+        tiles = pl.ds(first(g), PART)
+        for j in range(2):
+            a, b = sums(rows_of, slice(128 * j, 128 * (j + 1)))
+            tile0 = jnp.where(upper, a, pltpu.roll(b, 4, 1))
+            tile1 = jnp.where(upper, pltpu.roll(a, 4, 1), b)
+            mine[2 * half + j, tiles] = jnp.where(core == 0, tile0, tile1)
+            give[2 * half + j, tiles] = jnp.where(core == 0, tile1, tile0)
+
+    everything = pl.ds(0, PLACES)
+
+    for k in range(CHUNKS):
+        dress(k)
+    dress_rest()
+
+    for copy in small[4:]:
+        copy.wait()
 
     row_index = []
     lane = lax.broadcasted_iota(I32, (GROUPS, ROWS), 1)
@@ -211,172 +383,6 @@
         slab_send[:, kk, 128:384] = jnp.where(core == 0, value, 0.0)
         slab_send[:, 4 + kk, 128:384] = jnp.where(core == 0, 0.0, value)
 
-    def gathered(index):
-        hit = (lax.broadcasted_iota(I32, (index.shape[0], 1024), 1) == index).astype(BF16)
-        return jnp.dot(hit, table[...], preferred_element_type=F32).astype(BF16)
-
-    def dressed(k, select_i, select_j):
-        left = jnp.dot(orbits[0, k], select_i, preferred_element_type=F32)
-        right = jnp.dot(orbits[1, k], select_j, preferred_element_type=F32)
-        return t2[k] + left * right
-
-    in_chunk = lax.broadcasted_iota(I32, (CHUNK, ROWS), 0)
-
-    def dress(k):
-        if k + 2 < CHUNKS:
-            load_t2(k + 2).start()
-        load_w(k).start()
-        load_t2(k).wait()
-        index = pair[k]
-        orbits[0, k] = gathered(index[:, 0:1])
-        orbits[1, k] = gathered(index[:, 1:2])
-        in_a = k <= mixed
-        value = dressed(
-            k,
-            jnp.where(in_a, select[0, 0], select[1, 0]),
-            jnp.where(in_a, select[0, 1], select[1, 1]),
-        )
-        bound = jnp.where(k > mixed, CHUNK, count - k * CHUNK)
-        d_high[k], d_low[k] = split(jnp.where(in_chunk < bound, value, 0.0))
-
-    def dress_rest():
-        value = dressed(mixed, select[1, 0], select[1, 1])
-        value = jnp.where(in_chunk < count - mixed * CHUNK, 0.0, value)
-        d_high[CHUNKS], d_low[CHUNKS] = split(value)
-
-    def product(k, n, half):
-        columns = pl.ds(pl.multiple_of(half * WIDE, WIDE), WIDE)
-        w_high, w_low = split(w[n, :, columns])
-        return (
-            over_rows(d_high[k], w_high) + over_rows(d_high[k], w_low) + over_rows(d_low[k], w_high)
-        )
-
-    def multiply(k, half):
-        parts[k] = product(k, k, half)
-
-    def sums(rows_of, columns):
-        a = jnp.zeros((8 * PART, 128), F32)
-        b = parts[CHUNKS, rows_of, columns]
-        for k in range(CHUNKS):
-            part = parts[k, rows_of, columns]
-            a += part * jnp.where(k <= mixed, 1.0, 0.0)
-            b += part * jnp.where(k > mixed, 1.0, 0.0)
-        return a.reshape(PART, 8, 128), b.reshape(PART, 8, 128)
-
-    def h1_copy(d):
-        to = lax.rem(z + d, NZ)
-        return pltpu.make_async_remote_copy(
-            src_ref=slab_send.at[to],
-            dst_ref=slab_recv.at[z],
-            send_sem=hole_sems.at[0, 0],
-            recv_sem=hole_sems.at[1, 0],
-            device_id=device(to * NY + y, core),
-            device_id_type=MESH,
-        )
-
-    def h2_copy(d):
-        other = lax.rem(y * 2 + core + d, 2 * NY)
-        return pltpu.make_async_remote_copy(
-            src_ref=slab_recv.at[:, :, pl.ds(0, 128)],
-            dst_ref=slab_all.at[core, :, y],
-            send_sem=hole_sems.at[0, 1],
-            recv_sem=hole_sems.at[1, 1],
-            device_id=(z * 2 * NY + other, x),
-            device_id_type=MESH,
-        )
-
-    def h3_copy(d):
-        to = lax.rem(z + d, NZ)
-        return pltpu.make_async_remote_copy(
-            src_ref=hole_send.at[to],
-            dst_ref=hole_recv.at[z],
-            send_sem=hole_sems.at[0, 2],
-            recv_sem=hole_sems.at[1, 2],
-            device_id=device(to * NY + y, core),
-            device_id_type=MESH,
-        )
-
-    def wait_bytes(ref, sem):
-        pltpu.make_async_copy(ref, ref, sem).wait()
-
-    def h1_wait(end):
-        wait_bytes(slab_recv.at[pl.ds(0, NZ - 1)], hole_sems.at[end, 0])
-
-    def h2_wait(end):
-        wait_bytes(slab_all.at[:, pl.ds(0, NZ - 1)], hole_sems.at[end, 1])
-
-    def h3_wait(end):
-        wait_bytes(hole_recv.at[pl.ds(0, NZ - 1)], hole_sems.at[end, 2])
-
-    own = x // 2
-    far = 1 - own
-    odd = lax.rem(x, 2)
-    way_far = 1 - odd
-    way_own = odd
-    to_far = jnp.where(odd == 0, xm, xp)
-    to_own = jnp.where(odd == 0, xp, xm)
-
-    def first(g):
-        return lax.rem(z // 2 + 1 + g, PARTS) * PART
-
-    def core_copy(half, tiles, n):
-        part = (pl.ds(2 * half, 2), tiles)
-        return pltpu.make_async_remote_copy(
-            src_ref=give.at[part],
-            dst_ref=got.at[part],
-            send_sem=core_sems.at[0, n],
-            recv_sem=core_sems.at[1, n],
-            device_id=device(place, 1 - core),
-            device_id_type=MESH,
-        )
-
-    def ring1_copy(way):
-        return pltpu.make_async_remote_copy(
-            src_ref=mine.at[xo, pl.ds(HALF * way, HALF)],
-            dst_ref=ring1.at[way],
-            send_sem=ring_sems.at[0, 0],
-            recv_sem=ring_sems.at[1, 1 + way],
-            device_id=(virt, xp if way == 0 else xm),
-            device_id_type=MESH,
-        )
-
-    def ring2_copy(way, to, tiles, recv_sem):
-        return pltpu.make_async_remote_copy(
-            src_ref=mine.at[to, tiles],
-            dst_ref=ring2.at[way, tiles],
-            send_sem=ring_sems.at[0, 0],
-            recv_sem=recv_sem,
-            device_id=(virt, to),
-            device_id_type=MESH,
-        )
-
-    def all_copy(to):
-        return pltpu.make_async_remote_copy(
-            src_ref=mine.at[x, to],
-            dst_ref=recv.at[place],
-            send_sem=all_sems.at[0],
-            recv_sem=all_sems.at[1],
-            device_id=device(to, core),
-            device_id_type=MESH,
-        )
-
-    upper = lax.broadcasted_iota(I32, (PART, 8, 128), 1) < 4
-
-    def assemble(half, g):
-        rows_of = pl.ds(pl.multiple_of(first(g) * 8, 8 * PART), 8 * PART)
-        tiles = pl.ds(first(g), PART)
-        for j in range(2):
-            a, b = sums(rows_of, slice(128 * j, 128 * (j + 1)))
-            tile0 = jnp.where(upper, a, pltpu.roll(b, 4, 1))
-            tile1 = jnp.where(upper, pltpu.roll(a, 4, 1), b)
-            mine[2 * half + j, tiles] = jnp.where(core == 0, tile0, tile1)
-            give[2 * half + j, tiles] = jnp.where(core == 0, tile1, tile0)
-
-    everything = pl.ds(0, PLACES)
-
-    for k in range(CHUNKS):
-        dress(k)
-    dress_rest()
     pl.semaphore_wait(barrier, 2 + PLACES - 1 + 1 + NY - 1)
     for d in range(1, NZ):
         h1_copy(d).start()

time: 34.9 us -> 35 us (level)
  no operation moved by 1% of the time
where the time goes in v5:
time: 35 us; the launch traced here: 34.9 us
  Pallas kernels  34.3 us (98%)
  local copies, waits for them, and re-layouts  0.61 us (2%)
    pallas_call x1, Pallas kernels, body(): pl.pallas_call(ladder_kernel, out_shape=pltpu.VMEM((GROUPS, 4, 128), F32)...  34.3 us

profile of v5, /device:TPU:2, one launch (start us, length us, event | category | flops | bytes accessed | tf_op | source)
XLA Modules:
  0.0 34.9 jit_solution(11998510714060327976)
XLA Ops:
  0.0 34.3 %ladder.1 = f32[8,4,128]{2,1,0:T(4,128)S(1)} custom-call(s32[8]{0:T(128)} %starts_hbm.1, f32[120,960]{1,0:T(8,128)} %singles_hbm.1, s32[2,3600]{1,0:T(2,128)} %pairs_hbm.1, s32[8,2,256]{2,1,0:T(2,128)} %bitcast.10, s32[8,2,128]{2,1,0:T(2,128)} %bitcast.11, f32[8,4,128]{2,1,0:T(4,128)} %slab_hbm.1, f32[8,4,256]{2,1,0:T(4,128)} %hole_hbm.1, ...), custom_call_target="tpu_custom_call" | custom-call | tf_op jit(solution)/shard_map/ladder/pallas_call | solution.py:508
  34.3 0.6 %copy.14 = f32[8,4,128]{2,1,0:T(4,128)} copy(f32[8,4,128]{2,1,0:T(4,128)S(1)} %ladder.1) | data formatting | bytes 32768
